TPU v7x, 32 devices: a whole 2x2x4 slice. The times are simulated.
32 devices in a mesh: region: 2 (over core), tile: 16 (over z, y, x).
Axes of the slice: x: 2, y: 2, z: 4, core: 2. Of those that a mesh axis runs over, the one named last changes fastest.
Arguments:
- ens_obs: bfloat16 [4096, 512], P(('region', 'tile')), may hold values from -6 to 6
- obs_values: float32 [4096], P(('region', 'tile')), may hold values from -8 to 8
- obs_var: float32 [4096], P(('region', 'tile')), may hold values from 0.25 to 4
- edge_up: int32 [1024], P(('region', 'tile')), may hold values from 0 to 127
- edge_down: int32 [1024], P(('region', 'tile')), may hold values from 0 to 127
- loc_local: float32 [64, 2048], P(('region', 'tile')), may hold values from 0.02 to 1
- loc_edge: float32 [64, 1024], P(('region', 'tile')), may hold values from 0.02 to 1
- states: bfloat16 [2, 8192, 512], P(None, ('region', 'tile')), may hold values from -6 to 6
- box_ids: int32 [8192], P(('region', 'tile')), may hold values from 0 to 1
Outputs:
- analysis: bfloat16 [2, 8192, 512], P(None, ('region', 'tile'))
All inputs are finite; a program needn't handle non-finite values.
Results may differ from a plain program's by a relative error of at most 0.0095.
Values may be sent and summed in bfloat16 or wider, within the bound.
A program may use at most 128 MiB of HBM per device.

v0:
```python
import jax
import jax.numpy as jnp
from jax import lax
from jax.sharding import PartitionSpec as P


def passed_along(block, axis, distance):
    devices = range(lax.axis_size(axis))
    route = [(i - distance, i) for i in devices if i - distance in devices]
    return lax.ppermute(block, axis, route)


def obs_terms(anomaly, obs_info, weights):
    obs_scale = weights * obs_info[:, 0].astype(jnp.float32)[None, :]
    scaled = (anomaly[None] * obs_scale[:, :, None]).astype(jnp.bfloat16)
    gram_sum = jnp.einsum("bpi,pj->bij", scaled, anomaly, preferred_element_type=jnp.float32)
    weighted = (obs_scale * obs_info[:, 1].astype(jnp.float32)[None, :]).astype(jnp.bfloat16)
    innov_sum = jnp.einsum("bp,pj->bj", weighted, anomaly, preferred_element_type=jnp.float32)
    return (gram_sum, innov_sum)


def solve_one(chol_part, rhs_part):
    return jax.scipy.linalg.cho_solve((chol_part, True), rhs_part)


def make_transform(gram_sum, innov_sum):
    members = gram_sum.shape[-1]
    identity = jnp.eye(members, dtype=jnp.float32)
    system = gram_sum + (members - 1.0) * identity
    factor = jnp.linalg.cholesky(system)
    right_sides = jnp.concatenate(
        [jnp.broadcast_to(identity, system.shape), innov_sum[:, :, None]], axis=2
    )
    solved = jax.vmap(solve_one)(factor, right_sides)
    inverse = solved[:, :, :members]
    wbar = solved[:, :, members]
    transform = 0.5 * identity + 0.5 * (members - 1.0) * inverse + wbar[:, :, None]
    return transform.astype(jnp.bfloat16)


def body(ens_obs, obs_values, obs_var, edge_up, edge_down, loc_local, loc_edge, states, box_ids):
    record_count = ens_obs.shape[0]
    members = ens_obs.shape[1]
    ymean = jnp.mean(ens_obs, axis=1, dtype=jnp.float32)
    anomaly = (ens_obs.astype(jnp.float32) - ymean[:, None]).astype(jnp.bfloat16)
    obs_info = jnp.stack([1.0 / obs_var, obs_values - ymean], axis=1).astype(jnp.bfloat16)
    lower_a, lower_i = passed_along((anomaly[edge_up], obs_info[edge_up]), "region", 1)
    upper_a, upper_i = passed_along((anomaly[edge_down], obs_info[edge_down]), "region", -1)
    edge_anom = jnp.concatenate([lower_a, upper_a], axis=0)
    edge_info = jnp.concatenate([lower_i, upper_i], axis=0)
    block_anom = jnp.concatenate([anomaly, edge_anom], axis=0)
    block_info = jnp.concatenate([obs_info, edge_info], axis=0)
    all_anom, all_info = (
        lax.all_gather(block_anom, "tile", axis=0, tiled=True),
        lax.all_gather(block_info, "tile", axis=0, tiled=True),
    )
    tile_count = lax.axis_size("tile")
    pool_rows = block_anom.shape[0]
    all_anom = all_anom.reshape(tile_count, pool_rows, members)
    all_info = all_info.reshape(tile_count, pool_rows, 2)
    gram_one, innov_one = obs_terms(
        all_anom[:, :record_count].reshape(-1, members),
        all_info[:, :record_count].reshape(-1, 2),
        loc_local,
    )
    gram_two, innov_two = obs_terms(
        all_anom[:, record_count:].reshape(-1, members),
        all_info[:, record_count:].reshape(-1, 2),
        loc_edge,
    )
    transform = make_transform(gram_one + gram_two, innov_one + innov_two)
    smean = jnp.mean(states, axis=2, dtype=jnp.float32)
    state_anomaly = (states.astype(jnp.float32) - smean[:, :, None]).astype(jnp.bfloat16)
    updates = jnp.einsum(
        "fck,bkj->bfcj", state_anomaly, transform, preferred_element_type=jnp.float32
    )
    box_range = jnp.arange(transform.shape[0], dtype=jnp.int32)
    selector = (box_ids[None, :] == box_range[:, None]).astype(jnp.float32)
    total = jnp.sum(selector[:, None, :, None] * updates, axis=0)
    return (smean[:, :, None] + total).astype(jnp.bfloat16)


def solution(mesh):
    return jax.shard_map(
        body,
        mesh=mesh,
        in_specs=(
            P(("region", "tile"), None),
            P(("region", "tile")),
            P(("region", "tile")),
            P(("region", "tile")),
            P(("region", "tile")),
            P(("region", "tile"), None),
            P(("region", "tile"), None),
            P(None, ("region", "tile"), None),
            P(("region", "tile")),
        ),
        out_specs=P(None, ("region", "tile"), None),
        check_vma=False,
    )
```

profile of v0, /device:TPU:0, one launch (start us, length us, event | category | flops | bytes accessed | tf_op | source)
XLA Modules:
  0.0 424.2 jit_solution(17334717168470132983)
XLA Ops:
  10.5 2.4 collective-permute-start
  13.5 1.4 collective-permute-start.1
  15.0 1.8 collective-permute-done.1
  18.9 2.1 collective-permute-start.2
  21.6 1.3 collective-permute-start.3
  23.0 1.4 copy.133
  29.1 1.3 copy.142
  30.4 1.3 copy.123
  32.0 41.9 %all-gather = bf16[16,192,2]{1,2,0:T(2,128)(2,1)S(1)} all-gather(bf16[1,192,2]{1,2,0:T(2,128)(2,1)S(1)} %maximum_bitcast_fusion), channel_id=1, replica_groups=mesh['region'=2,'tile'=16] {'tile'}, dimensions={0}, use_global_device_ids=true | all-gather | bytes 13056 | tf_op jit(solution)/shard_map/all_gather | solution.py:55
  75.3 12.7 %all-gather.3.cloned.1.call-done = bf16[3072,512]{1,0:T(8,128)(2,1)} async-done(((bf16[192,512]{1,0:T(8,128)(2,1)}), bf16[3072,512]{1,0:T(8,128)(2,1)}) %all-gather.3.cloned.1.call-update) | async-done | bytes 3145744 | tf_op jit(solution)/shard_map/all_gather | solution.py:54
  88.0 1.3 slice.211
  89.3 1.8 slice.208
  91.1 1.7 bitcast_convert_fusion
  92.8 3.4 copy.129
  96.2 2.7 bitcast_convert_fusion.1
  98.9 5.4 %copy.124 = f32[2048,512]{0,1:T(8,128)} copy(f32[2048,512]{1,0:T(8,128)} %bitcast_convert_fusion.1) | data formatting | bytes 8388608 | tf_op jit(solution)/shard_map/convert_element_type | solution.py:15
  104.4 3.0 fusion.3
  107.5 4.3 %broadcast_add_fusion = (f32[2,512,512]{1,2,0:T(8,128)}, f32[2,512,512]{1,2,0:T(8,128)}) fusion(f32[512,512]{0,1:T(8,128)S(1)} %copy-done.10, f32[2,512,512]{1,2,0:T(8,128)S(1)} %fusion.3, bf16[2048,512,1]{1,0,2:T(8,128)(2,1)S(1)} %bitcast.110, f32[2,2048]{1,0:T(2,128)S(1)} %broadcast_multiply_fusion, f32[2048,512]{0,1:T(8,128)S(1)} %copy-done.4), kind=kOutput, calls=%fused_computation.70 | convolution fusion | flops 2152726528 | bytes 13647872 | tf_op jit(solution)/shard_map/bpi,pj->bij/dot_general | solution.py:16
  111.8 2.9 copy.134
  114.7 3.1 fusion.8
  117.8 1.3 copy-done.2
  119.2 23.5 %custom-call.38 = f32[2,128,128]{2,1,0:T(8,128)S(1)} custom-call(f32[2,128,128]{2,1,0:T(8,128)S(1)} %cholesky.274), custom_call_target="Cholesky" | custom-call | tf_op jit(solution)/shard_map/jit(cholesky)/cholesky | solution.py:30
  142.7 1.6 cholesky.234
  144.2 19.8 %custom-call.39 = f32[2,1,128,128]{2,3,1,0:T(8,128)S(1)} custom-call(f32[2,1,128,128]{3,2,1,0:T(8,128)S(1)} %select_bitcast_fusion.2), custom_call_target="InvertDiagBlocksLowerTriangular" | custom-call | tf_op jit(solution)/shard_map/jit(cholesky)/cholesky | solution.py:30
  164.1 2.3 constant_dynamic-update-slice_fusion.3
  166.4 1.5 convolution_subtract_fusion.4
  168.5 24.9 %custom-call.40 = f32[2,128,128]{2,1,0:T(8,128)} custom-call(f32[2,128,128]{2,1,0:T(8,128)} %cholesky.278), custom_call_target="Cholesky" | custom-call | tf_op jit(solution)/shard_map/jit(cholesky)/cholesky | solution.py:30
  193.4 1.6 select_bitcast_fusion.1
  195.1 21.1 %custom-call.41 = f32[2,1,128,128]{2,3,1,0:T(8,128)} custom-call(f32[2,1,128,128]{3,2,1,0:T(8,128)} %get-tuple-element.30), custom_call_target="InvertDiagBlocksLowerTriangular" | custom-call | tf_op jit(solution)/shard_map/jit(cholesky)/cholesky | solution.py:30
  216.2 2.0 convolution_dynamic-update-slice_fusion
  218.2 1.8 convolution_subtract_fusion.5
  220.7 24.9 %custom-call.42 = f32[2,128,128]{2,1,0:T(8,128)} custom-call(f32[2,128,128]{2,1,0:T(8,128)} %cholesky.283), custom_call_target="Cholesky" | custom-call | tf_op jit(solution)/shard_map/jit(cholesky)/cholesky | solution.py:30
  245.6 1.6 select_bitcast_fusion
  247.2 21.3 %custom-call.43 = f32[2,1,128,128]{2,3,1,0:T(8,128)} custom-call(f32[2,1,128,128]{3,2,1,0:T(8,128)} %get-tuple-element.28), custom_call_target="InvertDiagBlocksLowerTriangular" | custom-call | tf_op jit(solution)/shard_map/jit(cholesky)/cholesky | solution.py:30
  268.5 1.8 convolution_dynamic-update-slice_fusion.1
  270.4 1.8 convolution_subtract_fusion.6
  272.2 23.5 %custom-call.44 = f32[2,128,128]{2,1,0:T(8,128)S(1)} custom-call(f32[2,128,128]{2,1,0:T(8,128)S(1)} %convolution_subtract_fusion.6), custom_call_target="Cholesky" | custom-call | tf_op jit(solution)/shard_map/jit(cholesky)/cholesky | solution.py:30
  295.6 1.7 select_reduce_fusion.2
  297.9 3.4 select_select_fusion
  301.3 13.7 %while.1 = (s32[]{:T(128)}, f32[2,512,512]{2,1,0:T(8,128)}, s32[4,2]{0,1:T(2,128)S(1)}, f32[4,2,128,128]{3,2,0,1:T(8,128)}, s32[]{:T(128)}) while((s32[]{:T(128)}, f32[2,512,512]{2,1,0:T(8,128)}, s32[4,2]{0,1:T(2,128)S(1)}, f32[4,2,128,128]{3,2,0,1:T(8,128)}, s32[]{:T(128)}) %tuple.31), condition=%wide.while_cond, body=%wide.while_body.sunk | while | flops 2 | bytes 263777 | solution.py:23
  301.9 2.8 bitcast_dynamic-update-slice_fusion.2
  305.3 2.8 bitcast_dynamic-update-slice_fusion.2
  308.7 2.8 bitcast_dynamic-update-slice_fusion.2
  312.2 2.8 bitcast_dynamic-update-slice_fusion.2
  314.9 80.4 %custom-call.45 = f32[2,4,128,128]{2,3,1,0:T(8,128)} custom-call(f32[2,4,128,128]{3,2,1,0:T(8,128)} %bitcast.121), custom_call_target="InvertDiagBlocksLowerTriangular" | custom-call | tf_op jit(solution)/shard_map/vmap(jit(_cho_solve))/triangular_solve | solution.py:23
  402.6 1.9 fusion.27
  408.6 1.3 convolution_subtract_fusion
  410.9 1.9 fusion.24
  (126 shorter events, 34.5 us)
Async XLA Ops:
  6.5 81.4 %all-gather.3.cloned.1.call-start = ((), (), s32[]{:S(2)}) async-start(), calls=%async_computation | async-start | bytes 3342336 | tf_op jit(solution)/shard_map/all_gather | solution.py:54
  10.5 4.5 %collective-permute-start = (bf16[32,512]{1,0:T(8,128)(2,1)S(1)}, bf16[32,512]{1,0:T(8,128)(2,1)S(1)}, u32[]{:S(2)}, u32[]{:S(2)}) collective-permute-start(bf16[32,512]{1,0:T(8,128)(2,1)S(1)} %gather_fusion), channel_id=1, source_target_pairs={{0,16},{1,17},{2,18},{3,19},{4,20},{5,21},{6,22},{7,23},{8,24},{9,... | collective-permute-start | bytes 98312 | tf_op jit(solution)/shard_map/ppermute | solution.py:10
  13.5 12.8 %copy-start.5 = (bf16[2,256,512]{2,1,0:T(8,128)(2,1)S(1)}, bf16[2,256,512]{2,1,0:T(8,128)(2,1)}, u32[]{:S(2)}) copy-start(bf16[2,256,512]{2,1,0:T(8,128)(2,1)} %param.16) | copy-start | bytes 1572868
  13.5 3.2 collective-permute-start.1
  18.9 12.8 %collective-permute-start.2 = (bf16[32,2]{1,0:T(8,128)(2,1)S(1)}, bf16[32,2]{1,0:T(8,128)(2,1)S(1)}, u32[]{:S(2)}, u32[]{:S(2)}) collective-permute-start(bf16[32,2]{1,0:T(8,128)(2,1)S(1)} %gather_fusion.2), channel_id=1, source_target_pairs={{0,16},{1,17},{2,18},{3,19},{4,20},{5,21},{6,22},{7,23},{8,24},{9,... | collective-permute-start | bytes 392 | tf_op jit(solution)/shard_map/ppermute | solution.py:10
  21.6 10.2 %collective-permute-start.3 = (bf16[32,2]{1,0:T(8,128)(2,1)S(1)}, bf16[32,2]{1,0:T(8,128)(2,1)S(1)}, u32[]{:S(2)}, u32[]{:S(2)}) collective-permute-start(bf16[32,2]{1,0:T(8,128)(2,1)S(1)} %gather_fusion.3), channel_id=1, source_target_pairs={{16,0},{17,1},{18,2},{19,3},{20,4},{21,5},{22,6},{23,7},{24,8},{25... | collective-permute-start | bytes 392 | tf_op jit(solution)/shard_map/ppermute | solution.py:10
  24.4 3.5 copy-start.21
  29.1 45.5 %copy-start.20 = (f32[2,1024]{1,0:T(2,128)S(1)}, f32[2,1024]{1,0:T(2,128)}, u32[]{:S(2)}) copy-start(f32[2,1024]{1,0:T(2,128)} %param.15) | copy-start | bytes 24580
  29.1 46.2 %copy-start.19 = (f32[2,2048]{1,0:T(2,128)S(1)}, f32[2,2048]{1,0:T(2,128)}, u32[]{:S(2)}) copy-start(f32[2,2048]{1,0:T(2,128)} %param.14) | copy-start | bytes 49156
  74.6 29.7 %copy-start.13 = (f32[2,1024]{1,0:T(2,128)}, f32[2,1024]{1,0:T(2,128)S(1)}, u32[]{:S(2)}) copy-start(f32[2,1024]{1,0:T(2,128)S(1)} %broadcast_multiply_fusion.1) | copy-start | bytes 24580
  75.3 32.1 %copy-start.11 = (f32[2,2048]{1,0:T(2,128)}, f32[2,2048]{1,0:T(2,128)S(1)}, u32[]{:S(2)}) copy-start(f32[2,2048]{1,0:T(2,128)S(1)} %broadcast_multiply_fusion) | copy-start | bytes 49156
  104.4 3.1 copy-start.4
  104.4 3.1 copy-start.10
  117.8 1.3 copy-start.2
  142.6 23.7 %copy-start.8 = (f32[2,128,128]{2,1,0:T(8,128)}, f32[2,128,128]{2,1,0:T(8,128)S(1)}, u32[]{:S(2)}) copy-start(f32[2,128,128]{2,1,0:T(8,128)S(1)} %custom-call.38) | copy-start | bytes 393220
  218.2 77.4 %copy-start.9 = (f32[2,128,128]{2,1,0:T(8,128)S(1)}, f32[2,128,128]{2,1,0:T(8,128)}, u32[]{:S(2)}) copy-start(f32[2,128,128]{2,1,0:T(8,128)} %copy-done.8) | copy-start | bytes 393220
  297.8 3.4 copy-start.22
  297.9 97.5 %copy-start.12 = (f32[2,2048]{1,0:T(2,128)S(1)}, f32[2,2048]{1,0:T(2,128)}, u32[]{:S(2)}) copy-start(f32[2,2048]{1,0:T(2,128)} %copy-done.11) | copy-start | bytes 49156
  297.9 97.5 %copy-start.15 = (f32[2048,1]{0,1:T(1,128)S(1)}, f32[2048,1]{0,1:T(1,128)}, u32[]{:S(2)}) copy-start(f32[2048,1]{0,1:T(1,128)} %get-tuple-element.32) | copy-start | bytes 24580
  301.2 94.5 %copy-start.14 = (f32[2,1024]{1,0:T(2,128)S(1)}, f32[2,1024]{1,0:T(2,128)}, u32[]{:S(2)}) copy-start(f32[2,1024]{1,0:T(2,128)} %copy-done.13) | copy-start | bytes 24580
  301.2 94.5 %copy-start.18 = (f32[1024,1]{0,1:T(1,128)S(1)}, f32[1024,1]{0,1:T(1,128)}, u32[]{:S(2)}) copy-start(f32[1024,1]{0,1:T(1,128)} %get-tuple-element.34) | copy-start | bytes 12292
  395.4 1.2 copy-start.3
  395.8 1.1 copy-start.7
  396.9 1.6 copy-start.1
  413.8 1.2 copy-start
  413.8 1.3 copy-start.6
  413.8 1.3 copy-start.16
  413.8 1.3 copy-start.17
Sparse Core Ops, SparseCore 0:
  17.6 70.2 all-gather.2
where the time goes:
time: 428 us; the launch traced here: 424 us
  other arithmetic  267 us (62%)
  local copies, waits for them, and re-layouts  43.4 us (10%)
  blocking collectives  41.9 us (10%)
  matrix products  36.2 us (8%)
  waiting for transfers between devices  14.5 us (3%)
  between operations  14.1 us (3%)
  starting transfers between devices  7.13 us (2%)
    another operation x18, other arithmetic, make_transform(): factor = jnp.linalg.cholesky(system)  165 us
    another operation x5, other arithmetic, solve_one(): return jax.scipy.linalg.cho_solve((chol_part, True), rhs_part)  85.3 us
    all_gather x1, blocking collectives, body(): lax.all_gather(block_info, 'tile', axis=0, tiled=True)  41.9 us
    another operation x14, matrix products, solve_one(): return jax.scipy.linalg.cho_solve((chol_part, True), rhs_part)  16.2 us
    another operation x12, local copies, waits for them, and re-layouts  13.7 us
    all_gather x1, waiting for transfers between devices, body(): lax.all_gather(block_anom, 'tile', axis=0, tiled=True)  12.7 us
    another operation x6, matrix products, make_transform(): factor = jnp.linalg.cholesky(system)  11.2 us
    convert_element_type x2, local copies, waits for them, and re-layouts, obs_terms(): scaled = (anomaly[None] * obs_scale[:, :, None]).astype(jnp.bfloat16)  8.85 us
  transfers between devices with their start and end apart: 5, of which 2 were waited for; matrix products, arithmetic and copies ran while one was open for 3% of the time, Pallas kernels for 0%

commit v1 on v0

--- a/solution.py
+++ b/solution.py
@@ -1,6 +1,8 @@
 import jax
 import jax.numpy as jnp
 from jax import lax
+from jax.experimental import pallas as pl
+from jax.experimental.pallas import tpu as pltpu
 from jax.sharding import PartitionSpec as P
 
 
@@ -19,23 +21,110 @@
     return (gram_sum, innov_sum)
 
 
-def solve_one(chol_part, rhs_part):
-    return jax.scipy.linalg.cho_solve((chol_part, True), rhs_part)
+def split(x):
+    high = x.astype(jnp.bfloat16)
+    return high, (x - high.astype(jnp.float32)).astype(jnp.bfloat16)
 
 
-def make_transform(gram_sum, innov_sum):
-    members = gram_sum.shape[-1]
-    identity = jnp.eye(members, dtype=jnp.float32)
-    system = gram_sum + (members - 1.0) * identity
-    factor = jnp.linalg.cholesky(system)
-    right_sides = jnp.concatenate(
-        [jnp.broadcast_to(identity, system.shape), innov_sum[:, :, None]], axis=2
-    )
-    solved = jax.vmap(solve_one)(factor, right_sides)
-    inverse = solved[:, :, :members]
-    wbar = solved[:, :, members]
-    transform = 0.5 * identity + 0.5 * (members - 1.0) * inverse + wbar[:, :, None]
-    return transform.astype(jnp.bfloat16)
+def dot_once(left, right):
+    return jnp.dot(left.astype(jnp.bfloat16), right.astype(jnp.bfloat16), preferred_element_type=jnp.float32)
+
+
+def dot_thrice(left, right):
+    left_high, left_low = split(left)
+    right_high, right_low = split(right)
+    mixed = jnp.dot(left_low, right_high, preferred_element_type=jnp.float32)
+    mixed += jnp.dot(left_high, right_low, preferred_element_type=jnp.float32)
+    return mixed + jnp.dot(left_high, right_high, preferred_element_type=jnp.float32)
+
+
+def dot_full(left, right):
+    return jnp.dot(left, right, precision=lax.Precision.HIGHEST, preferred_element_type=jnp.float32)
+
+
+def shrink(error):
+    return error * error / (2.0 - error * error)
+
+
+def analyse_kernel(gram_ref, innov_ref, states_ref, ids_ref, out_ref, system, guess):
+    boxes, members, _ = gram_ref.shape
+    fields, cells, _ = states_ref.shape
+    rows = lax.broadcasted_iota(jnp.int32, (members, members), 0)
+    columns = lax.broadcasted_iota(jnp.int32, (members, members), 1)
+    identity = (rows == columns).astype(jnp.float32)
+    ridge = members - 1.0
+
+    worst = jnp.float32(0.0)
+    errors = []
+    for b in range(boxes):
+        full = gram_ref[b] + ridge * identity
+        top = jnp.maximum(jnp.max(jnp.sum(jnp.abs(full), axis=0, keepdims=True)), ridge)
+        first = 2.0 / (top + ridge)
+        error = (top - ridge) / (top + ridge)
+        mu = 2.0 / (2.0 - error * error)
+        system[b] = full
+        guess[b] = (mu * first) * (2.0 * identity - first * full)
+        errors.append(shrink(error))
+        worst = jnp.maximum(worst, top / ridge)
+
+    def refine(dot):
+        def step(carried):
+            after = []
+            for b in range(boxes):
+                error = carried[b]
+                mu = 2.0 / (2.0 - error * error)
+                left = 2.0 * identity - dot(system[b], guess[b])
+                guess[b] = mu * dot(guess[b], left)
+                after.append(shrink(error))
+            return tuple(after)
+        return step
+
+    def above(limit, allowed):
+        def proceed(carried):
+            top = carried[0]
+            for error in carried[1:]:
+                top = jnp.maximum(top, error)
+            return jnp.logical_and(allowed, top > limit)
+        return proceed
+
+    easy = worst < 64.0
+    hard = worst > 2048.0
+    errors = lax.while_loop(above(0.005, easy), refine(dot_once), tuple(errors))
+    errors = tuple(jnp.maximum(error, 0.02) for error in errors)
+    errors = lax.while_loop(above(3e-4, jnp.logical_not(hard)), refine(dot_thrice), errors)
+    errors = lax.while_loop(above(1e-6, hard), refine(dot_full), errors)
+
+    wide = states_ref[...].astype(jnp.float32).reshape(fields * cells, members)
+    smean = jnp.sum(wide, axis=1, keepdims=True) * (1.0 / members)
+    anomaly = (wide - smean).astype(jnp.bfloat16)
+    here = lax.broadcasted_iota(jnp.int32, (cells, cells), 0) == lax.broadcasted_iota(jnp.int32, (cells, cells), 1)
+    spread = jnp.broadcast_to(ids_ref[...].astype(jnp.float32), (cells, cells))
+    ids = jnp.sum(jnp.where(here, spread, 0.0), axis=1, keepdims=True)
+    ids = jnp.concatenate([ids] * fields, axis=0)
+    total = jnp.zeros((fields * cells, members), jnp.float32)
+    for b in range(boxes):
+        inverse = guess[b]
+        wbar = jnp.sum(inverse * innov_ref[b:b + 1, :], axis=1, keepdims=True)
+        transform = (0.5 * identity + (0.5 * ridge) * inverse + wbar).astype(jnp.bfloat16)
+        update = jnp.dot(anomaly, transform, preferred_element_type=jnp.float32)
+        total = jnp.where(ids == float(b), update, total)
+    out_ref[...] = (smean + total).astype(jnp.bfloat16).reshape(fields, cells, members)
+
+
+def analyse(gram, innov, states, box_ids):
+    boxes, members, _ = gram.shape
+    return pl.pallas_call(
+        analyse_kernel,
+        out_shape=jax.ShapeDtypeStruct(states.shape, jnp.bfloat16),
+        in_specs=[pl.BlockSpec(memory_space=pltpu.VMEM)] * 4,
+        out_specs=pl.BlockSpec(memory_space=pltpu.VMEM),
+        scratch_shapes=[
+            pltpu.VMEM((boxes, members, members), jnp.float32),
+            pltpu.VMEM((boxes, members, members), jnp.float32),
+        ],
+        compiler_params=pltpu.CompilerParams(vmem_limit_bytes=48 * 1024 * 1024),
+        name="analyse",
+    )(gram, innov, states, box_ids.reshape(1, -1))
 
 
 def body(ens_obs, obs_values, obs_var, edge_up, edge_down, loc_local, loc_edge, states, box_ids):
@@ -68,16 +157,7 @@
         all_info[:, record_count:].reshape(-1, 2),
         loc_edge,
     )
-    transform = make_transform(gram_one + gram_two, innov_one + innov_two)
-    smean = jnp.mean(states, axis=2, dtype=jnp.float32)
-    state_anomaly = (states.astype(jnp.float32) - smean[:, :, None]).astype(jnp.bfloat16)
-    updates = jnp.einsum(
-        "fck,bkj->bfcj", state_anomaly, transform, preferred_element_type=jnp.float32
-    )
-    box_range = jnp.arange(transform.shape[0], dtype=jnp.int32)
-    selector = (box_ids[None, :] == box_range[:, None]).astype(jnp.float32)
-    total = jnp.sum(selector[:, None, :, None] * updates, axis=0)
-    return (smean[:, :, None] + total).astype(jnp.bfloat16)
+    return analyse(gram_one + gram_two, innov_one + innov_two, states, box_ids)
 
 
 def solution(mesh):

time: 428 us -> 142 us (0.33)
  the two profiles are of different devices: /device:TPU:0 before, /device:TPU:2 now
where the time goes in v1:
time: 142 us; the launch traced here: 141 us
  blocking collectives  36.6 us (26%)
  waiting for transfers between devices  27.6 us (19%)
  Pallas kernels  24.7 us (17%)
  local copies, waits for them, and re-layouts  16.2 us (11%)
  between operations  13.5 us (10%)
  other arithmetic  11.3 us (8%)
  starting transfers between devices  6.38 us (4%)
  matrix products  4.22 us (3%)
    all_gather x1, blocking collectives, body(): lax.all_gather(block_info, 'tile', axis=0, tiled=True)  36.6 us
    pallas_call x1, Pallas kernels, analyse(): pl.pallas_call(analyse_kernel, out_shape=jax.ShapeDtypeStruct(states.shap...  24.7 us
    all_gather x1, waiting for transfers between devices, body(): lax.all_gather(block_anom, 'tile', axis=0, tiled=True)  24.1 us
    convert_element_type x2, local copies, waits for them, and re-layouts, obs_terms(): scaled = (anomaly[None] * obs_scale[:, :, None]).astype(jnp.bfloat16)  8.3 us
    ppermute x4, starting transfers between devices, passed_along(): return lax.ppermute(block, axis, route)  6.38 us
    convert_element_type x2, other arithmetic, obs_terms(): scaled = (anomaly[None] * obs_scale[:, :, None]).astype(jnp.bfloat16)  4.39 us
    dot_general x2, matrix products, obs_terms(): jnp.einsum('bpi,pj->bij', scaled, anomaly, preferred_element_type=jnp.flo...  3.61 us
    ppermute x4, waiting for transfers between devices, passed_along(): return lax.ppermute(block, axis, route)  3.46 us
  transfers between devices with their start and end apart: 5, of which 3 were waited for; matrix products, arithmetic and copies ran while one was open for 4% of the time, Pallas kernels for 0%

profile of v1, /device:TPU:2, one launch (start us, length us, event | category | flops | bytes accessed | tf_op | source)
XLA Modules:
  0.0 140.5 jit_solution(9394261961379672941)
XLA Ops:
  6.5 0.0 all-gather.3.cloned.1.call-start
  6.5 0.7 compare_select_fusion.1
  7.2 1.0 convert_reduce_fusion
  8.2 0.7 convert_bitcast_fusion
  8.9 1.0 fusion.7
  9.9 0.6 gather_fusion
  10.5 1.7 %collective-permute-start = (bf16[32,512]{1,0:T(8,128)(2,1)S(1)}, bf16[32,512]{1,0:T(8,128)(2,1)S(1)}, u32[]{:S(2)}, u32[]{:S(2)}) collective-permute-start(bf16[32,512]{1,0:T(8,128)(2,1)S(1)} %gather_fusion), channel_id=1, source_target_pairs={{0,16},{1,17},{2,18},{3,19},{4,20},{5,21},{6,22},{7,23},{8,24},{9,... | collective-permute-start | bytes 98312 | tf_op jit(solution)/shard_map/ppermute | solution.py:12
  12.3 0.7 compare_select_fusion
  12.9 0.6 gather_fusion.1
  13.6 1.3 collective-permute-start.1
  14.9 0.0 collective-permute-done
  14.9 1.8 %collective-permute-done.1 = bf16[32,512]{1,0:T(8,128)(2,1)S(1)} collective-permute-done((bf16[32,512]{1,0:T(8,128)(2,1)S(1)}, bf16[32,512]{1,0:T(8,128)(2,1)S(1)}, u32[]{:S(2)}, u32[]{:S(2)}) %collective-permute-start.1) | collective-permute-done | bytes 32800 | tf_op jit(solution)/shard_map/ppermute | solution.py:12
  16.7 0.7 pad_maximum_fusion
  17.3 0.0 all-gather.3.cloned.1.call-update
  17.4 0.7 convert_bitcast_fusion.1
  18.0 0.1 copy.29
  18.2 0.6 gather_fusion.2
  18.8 2.1 %collective-permute-start.2 = (bf16[32,2]{1,0:T(8,128)(2,1)S(1)}, bf16[32,2]{1,0:T(8,128)(2,1)S(1)}, u32[]{:S(2)}, u32[]{:S(2)}) collective-permute-start(bf16[32,2]{1,0:T(8,128)(2,1)S(1)} %gather_fusion.2), channel_id=1, source_target_pairs={{0,16},{1,17},{2,18},{3,19},{4,20},{5,21},{6,22},{7,23},{8,24},{9,... | collective-permute-start | bytes 392 | tf_op jit(solution)/shard_map/ppermute | solution.py:12
  20.9 0.6 gather_fusion.3
  21.4 1.3 collective-permute-start.3
  22.7 0.0 collective-permute-done.2
  22.8 0.1 copy.31
  22.8 1.7 %collective-permute-done.3 = bf16[32,2]{1,0:T(8,128)(2,1)S(1)} collective-permute-done((bf16[32,2]{1,0:T(8,128)(2,1)S(1)}, bf16[32,2]{1,0:T(8,128)(2,1)S(1)}, u32[]{:S(2)}, u32[]{:S(2)}) %collective-permute-start.3) | collective-permute-done | bytes 160 | tf_op jit(solution)/shard_map/ppermute | solution.py:12
  24.5 0.1 copy.32
  24.6 0.1 maximum_bitcast_fusion
  24.7 36.6 %all-gather = bf16[16,192,2]{1,2,0:T(2,128)(2,1)S(1)} all-gather(bf16[1,192,2]{1,2,0:T(2,128)(2,1)S(1)} %maximum_bitcast_fusion), channel_id=1, replica_groups=mesh['region'=2,'tile'=16] {'tile'}, dimensions={0}, use_global_device_ids=true | all-gather | bytes 13056 | tf_op jit(solution)/shard_map/all_gather | solution.py:144
  61.3 0.1 reshape.67
  61.4 0.7 broadcast_multiply_fusion.1
  62.1 0.7 broadcast_multiply_fusion
  62.8 24.1 %all-gather.3.cloned.1.call-done = bf16[3072,512]{1,0:T(8,128)(2,1)} async-done(((bf16[192,512]{1,0:T(8,128)(2,1)}), bf16[3072,512]{1,0:T(8,128)(2,1)}) %all-gather.3.cloned.1.call-update) | async-done | bytes 3145744 | tf_op jit(solution)/shard_map/all_gather | solution.py:143
  87.0 1.3 slice.43
  88.3 1.8 %slice.40 = bf16[16,128,512]{2,1,0:T(8,128)(2,1)S(1)} slice(bf16[16,192,512]{2,1,0:T(8,128)(2,1)} %bitcast.34), slice={[0:16], [0:128], [0:512]} | slice | bytes 4194304 | tf_op jit(solution)/shard_map/slice | solution.py:151
  90.1 1.7 %bitcast_convert_fusion = f32[1024,512]{1,0:T(8,128)} fusion(bf16[16,64,512]{2,1,0:T(8,128)(2,1)S(1)} %slice.43), kind=kLoop, calls=%fused_computation.39 | loop fusion | flops 524288 | bytes 3145728 | tf_op jit(solution)/shard_map/convert_element_type | solution.py:17
  91.8 2.9 %copy.33 = f32[1024,512]{0,1:T(8,128)} copy(f32[1024,512]{1,0:T(8,128)} %bitcast_convert_fusion) | data formatting | bytes 4194304 | tf_op jit(solution)/shard_map/convert_element_type | solution.py:17
  94.7 2.7 %bitcast_convert_fusion.1 = f32[2048,512]{1,0:T(8,128)} fusion(bf16[16,128,512]{2,1,0:T(8,128)(2,1)S(1)} %slice.40), kind=kLoop, calls=%fused_computation.40 | loop fusion | flops 1048576 | bytes 6291456 | tf_op jit(solution)/shard_map/convert_element_type | solution.py:17
  97.4 5.4 %copy.28 = f32[2048,512]{0,1:T(8,128)} copy(f32[2048,512]{1,0:T(8,128)} %bitcast_convert_fusion.1) | data formatting | bytes 8388608 | tf_op jit(solution)/shard_map/convert_element_type | solution.py:17
  102.8 0.0 copy-start.3
  102.8 0.4 fusion.8
  103.2 1.2 copy-done.3
  104.4 1.2 fusion.3
  105.6 0.2 convolution_add_fusion.innov_ref
  105.9 0.7 copy-done.2
  106.6 0.0 copy-start
  106.6 0.0 copy-start.1
  106.6 2.4 %fusion.6.gram_ref = f32[2,512,512]{2,1,0:T(8,128)S(1)} fusion(f32[2,512,512]{2,1,0:T(8,128)S(1)} %fusion.3, bf16[2048,512,1]{1,0,2:T(8,128)(2,1)S(1)} %bitcast.30, f32[2,2048]{1,0:T(2,128)S(1)} %broadcast_multiply_fusion, f32[2048,512]{0,1:T(8,128)S(1)} %copy-done.2), kind=kOutput, calls=%fused_computation.12 | convolution fusion | flops 2152202240 | bytes 10502144 | tf_op jit(solution)/shard_map/bpi,pj->bij/dot_general | solution.py:18
  109.0 0.0 copy-done
  109.0 0.0 copy-done.1
  109.0 24.7 %analyse.1 = bf16[2,256,512]{2,1,0:T(8,128)(2,1)} custom-call(f32[2,512,512]{2,1,0:T(8,128)S(1)} %fusion.6.gram_ref, f32[2,512]{1,0:T(2,128)S(1)} %convolution_add_fusion.innov_ref, bf16[2,256,512]{2,1,0:T(8,128)(2,1)S(1)} %copy-done, s32[1,256]{1,0:T(1,128)S(1)} %bitcast.28), custom_call_target="tpu_custom_call" | custom-call | tf_op jit(solution)/shard_map/analyse/pallas_call | solution.py:116
  (9 shorter events, 0.1 us)
Async XLA Ops:
  6.5 80.4 %all-gather.3.cloned.1.call-start = ((), (), s32[]{:S(2)}) async-start(), calls=%async_computation | async-start | bytes 3342336 | tf_op jit(solution)/shard_map/all_gather | solution.py:143
  10.5 4.3 %collective-permute-start = (bf16[32,512]{1,0:T(8,128)(2,1)S(1)}, bf16[32,512]{1,0:T(8,128)(2,1)S(1)}, u32[]{:S(2)}, u32[]{:S(2)}) collective-permute-start(bf16[32,512]{1,0:T(8,128)(2,1)S(1)} %gather_fusion), channel_id=1, source_target_pairs={{0,16},{1,17},{2,18},{3,19},{4,20},{5,21},{6,22},{7,23},{8,24},{9,... | collective-permute-start | bytes 98312 | tf_op jit(solution)/shard_map/ppermute | solution.py:12
  13.6 3.1 %collective-permute-start.1 = (bf16[32,512]{1,0:T(8,128)(2,1)S(1)}, bf16[32,512]{1,0:T(8,128)(2,1)S(1)}, u32[]{:S(2)}, u32[]{:S(2)}) collective-permute-start(bf16[32,512]{1,0:T(8,128)(2,1)S(1)} %gather_fusion.1), channel_id=1, source_target_pairs={{16,0},{17,1},{18,2},{19,3},{20,4},{21,5},{22,6},{23,7},{24,8},{25... | collective-permute-start | bytes 98312 | tf_op jit(solution)/shard_map/ppermute | solution.py:12
  18.8 4.0 %collective-permute-start.2 = (bf16[32,2]{1,0:T(8,128)(2,1)S(1)}, bf16[32,2]{1,0:T(8,128)(2,1)S(1)}, u32[]{:S(2)}, u32[]{:S(2)}) collective-permute-start(bf16[32,2]{1,0:T(8,128)(2,1)S(1)} %gather_fusion.2), channel_id=1, source_target_pairs={{0,16},{1,17},{2,18},{3,19},{4,20},{5,21},{6,22},{7,23},{8,24},{9,... | collective-permute-start | bytes 392 | tf_op jit(solution)/shard_map/ppermute | solution.py:12
  21.4 3.1 %collective-permute-start.3 = (bf16[32,2]{1,0:T(8,128)(2,1)S(1)}, bf16[32,2]{1,0:T(8,128)(2,1)S(1)}, u32[]{:S(2)}, u32[]{:S(2)}) collective-permute-start(bf16[32,2]{1,0:T(8,128)(2,1)S(1)} %gather_fusion.3), channel_id=1, source_target_pairs={{16,0},{17,1},{18,2},{19,3},{20,4},{21,5},{22,6},{23,7},{24,8},{25... | collective-permute-start | bytes 392 | tf_op jit(solution)/shard_map/ppermute | solution.py:12
  102.8 1.6 %copy-start.3 = (f32[1024,512]{0,1:T(8,128)S(1)}, f32[1024,512]{0,1:T(8,128)}, u32[]{:S(2)}) copy-start(f32[1024,512]{0,1:T(8,128)} %copy.33) | copy-start | bytes 6291460
  104.4 2.2 %copy-start.2 = (f32[2048,512]{0,1:T(8,128)S(1)}, f32[2048,512]{0,1:T(8,128)}, u32[]{:S(2)}) copy-start(f32[2048,512]{0,1:T(8,128)} %copy.28) | copy-start | bytes 12582916
  106.6 2.4 %copy-start = (bf16[2,256,512]{2,1,0:T(8,128)(2,1)S(1)}, bf16[2,256,512]{2,1,0:T(8,128)(2,1)}, u32[]{:S(2)}) copy-start(bf16[2,256,512]{2,1,0:T(8,128)(2,1)} %states_ref.1) | copy-start | bytes 1572868
  106.6 2.4 %copy-start.1 = (s32[256]{0:T(256)S(1)}, s32[256]{0:T(256)}, u32[]{:S(2)}) copy-start(s32[256]{0:T(256)} %param.17) | copy-start | bytes 3076
Sparse Core Ops, SparseCore 0:
  17.5 69.4 all-gather.2

commit v2 on v1

--- a/solution.py
+++ b/solution.py
@@ -1,3 +1,4 @@
+import functools
 import jax
 import jax.numpy as jnp
 from jax import lax
@@ -6,19 +7,220 @@
 from jax.sharding import PartitionSpec as P
 
 
-def passed_along(block, axis, distance):
-    devices = range(lax.axis_size(axis))
-    route = [(i - distance, i) for i in devices if i - distance in devices]
-    return lax.ppermute(block, axis, route)
-
-
-def obs_terms(anomaly, obs_info, weights):
-    obs_scale = weights * obs_info[:, 0].astype(jnp.float32)[None, :]
-    scaled = (anomaly[None] * obs_scale[:, :, None]).astype(jnp.bfloat16)
-    gram_sum = jnp.einsum("bpi,pj->bij", scaled, anomaly, preferred_element_type=jnp.float32)
-    weighted = (obs_scale * obs_info[:, 1].astype(jnp.float32)[None, :]).astype(jnp.bfloat16)
-    innov_sum = jnp.einsum("bp,pj->bj", weighted, anomaly, preferred_element_type=jnp.float32)
-    return (gram_sum, innov_sum)
+INFO_ROWS = 16
+
+
+def tile_sides(tiles):
+    return 4, 2, tiles // 8
+
+
+def gather_kernel(regions, tiles, ens_ref, values_ref, var_ref, up_ref, down_ref, local_ref, edge_ref,
+                  gram_ref, innov_ref, pool, weights, leaving, arriving,
+                  send_sem, recv_sem, edge_send_sem, edge_recv_sem):
+    region = lax.axis_index("region")
+    tile = lax.axis_index("tile")
+    z_side, y_side, x_side = tile_sides(tiles)
+    plane = y_side * x_side
+    at_z, at_y, at_x = tile // plane, (tile // x_side) % y_side, tile % x_side
+    at = tile % plane
+    records, members = ens_ref.shape
+    boxes = local_ref.shape[0]
+    edges = up_ref.shape[1]
+    sides = leaving.shape[0]
+    rows = records + sides * edges
+    block_rows = pool.shape[2]
+    cut = (block_rows // 2 + 15) // 16 * 16
+
+    x_others = [at_y * x_side + (at_x + d) % x_side for d in range(1, x_side)]
+    y_others = [(at_y + d) % y_side * x_side + at_x for d in range(1, y_side)]
+    z_others = [(at_z + d) % z_side for d in range(1, z_side)]
+    if sides == 1:
+        partners = [(1 - region, 0)]
+    else:
+        partners = [((region + 1) % regions, 0), ((region + regions - 1) % regions, 1)]
+
+    barrier = pltpu.get_barrier_semaphore()
+    greeted = [(region, z * plane + at) for z in z_others]
+    greeted += [(region, at_z * plane + p) for p in x_others + y_others]
+    greeted += [(partner, tile) for partner, _ in partners]
+    for device in greeted:
+        pl.semaphore_signal(barrier, inc=1, device_id=device, device_id_type=pl.DeviceIdType.MESH)
+
+    wide = ens_ref[...].astype(jnp.float32)
+    ymean = jnp.sum(wide, axis=1, keepdims=True) * (1.0 / members)
+    anomaly = (wide - ymean).astype(jnp.bfloat16)
+    row_at = lax.broadcasted_iota(jnp.int32, (records, records), 0)
+    column_at = lax.broadcasted_iota(jnp.int32, (records, records), 1)
+    ymean_row = jnp.sum(jnp.where(row_at == column_at, ymean, 0.0), axis=0, keepdims=True)
+    info = jnp.concatenate(
+        [1.0 / var_ref[...], values_ref[...] - ymean_row, jnp.zeros((INFO_ROWS - 2, records), jnp.float32)], axis=0
+    ).astype(jnp.bfloat16)
+
+    def picked(index_row, keep):
+        index = jnp.concatenate([index_row] * (records // edges), axis=1)
+        chosen = jnp.where(row_at == index, keep, 0.0)
+        far_info = jnp.dot(info, chosen.astype(jnp.bfloat16), preferred_element_type=jnp.float32)
+        chosen = chosen.T[:edges].astype(jnp.bfloat16)
+        far = jnp.dot(chosen, anomaly, preferred_element_type=jnp.float32)
+        return far.astype(jnp.bfloat16), far_info.astype(jnp.bfloat16)
+
+    if sides == 1:
+        chosen_row = jnp.where(region == 0, up_ref[...], down_ref[...])
+        going = [picked(chosen_row, 1.0)]
+    else:
+        going = [
+            picked(up_ref[...], jnp.where(region == regions - 1, 0.0, 1.0)),
+            picked(down_ref[...], jnp.where(region == 0, 0.0, 1.0)),
+        ]
+    for side, (far, far_info) in enumerate(going):
+        leaving[side, :edges, :] = far
+        leaving[side, edges:, :records] = far_info
+        leaving[side, edges:, records:] = jnp.zeros((INFO_ROWS, members - records), jnp.bfloat16)
+    pool[at, at_z, :records, :] = anomaly
+
+    pl.semaphore_wait(barrier, len(greeted))
+    started = []
+    crossing = []
+    for partner, side in partners:
+        copy = pltpu.make_async_remote_copy(
+            src_ref=leaving.at[side], dst_ref=arriving.at[side],
+            send_sem=edge_send_sem.at[side], recv_sem=edge_recv_sem.at[side],
+            device_id=(partner, tile), device_id_type=pl.DeviceIdType.MESH,
+        )
+        copy.start()
+        crossing.append(copy)
+    for copy in crossing:
+        copy.wait_recv()
+    pieces = [info]
+    for side in range(sides):
+        pool[at, at_z, pl.ds(records + side * edges, edges), :] = arriving[side, :edges, :]
+        pieces.append(arriving[side, edges:, :edges])
+    pieces.append(jnp.zeros((INFO_ROWS, members - rows), jnp.bfloat16))
+    pool[at, at_z, rows:, :] = jnp.concatenate(pieces, axis=1)
+
+    def piece(place, z, part):
+        if part is None:
+            return pool.at[place, z]
+        if part == 0:
+            return pool.at[place, z, pl.ds(0, cut)]
+        return pool.at[place, z, pl.ds(cut, block_rows - cut)]
+
+    def describe(place, z, part, device, number):
+        return pltpu.make_async_remote_copy(
+            src_ref=piece(place, z, part), dst_ref=piece(place, z, part),
+            send_sem=send_sem.at[number], recv_sem=recv_sem.at[1 if part == 1 else 0, place, z],
+            device_id=device, device_id_type=pl.DeviceIdType.MESH,
+        )
+
+    def send(place, z, part, device):
+        copy = describe(place, z, part, device, len(started))
+        copy.start()
+        started.append(copy)
+
+    def await_piece(place, z, part=None):
+        describe(place, z, part, (region, tile), 0).wait_recv()
+
+    def spread(z):
+        for p in x_others + y_others:
+            send(at, z, None, (region, at_z * plane + p))
+
+    for z in z_others:
+        send(at, at_z, None, (region, z * plane + at))
+    spread(at_z)
+
+    edge_columns = 2 * edges
+    for t in range(tiles):
+        weights[t, :, :records] = local_ref[:, t * records:(t + 1) * records]
+        near = edge_ref[:, t * edge_columns:(t + 1) * edge_columns]
+        if sides == 1:
+            near = jnp.where(region == 0, near[:, edges:], near[:, :edges])
+        weights[t, :, records:rows] = near
+
+    def absorb(place, first=False):
+        block = pool[place]
+        data = jnp.concatenate(
+            [block[:, :records].reshape(z_side * records, members),
+             block[:, records:rows].reshape(z_side * (rows - records), members)], axis=0)
+        turned = data.astype(jnp.float32).T
+        inverse_var = [block[z, rows:, :rows].astype(jnp.float32)[0:1] for z in range(z_side)]
+        innovation = [block[z, rows:, :rows].astype(jnp.float32)[1:2] for z in range(z_side)]
+        loc = [weights[z * plane + place][:, :rows] for z in range(z_side)]
+
+        def ordered(parts):
+            return jnp.concatenate([p[:, :records] for p in parts] + [p[:, records:] for p in parts], axis=1)
+
+        scale = ordered(loc) * ordered(inverse_var)
+        weighted = (scale * ordered(innovation)).astype(jnp.bfloat16)
+        more = jnp.dot(weighted, data, preferred_element_type=jnp.float32)
+        innov_ref[...] = more if first else innov_ref[...] + more
+        for b in range(boxes):
+            scaled = (turned * scale[b:b + 1]).astype(jnp.bfloat16)
+            more = jnp.dot(scaled, data, preferred_element_type=jnp.float32)
+            gram_ref[b] = more if first else gram_ref[b] + more
+
+    order = [(at_z + z_side - d) % z_side for d in range(1, z_side)]
+    for z in order:
+        await_piece(at, z)
+        spread(z)
+    absorb(at, first=True)
+    for z in [at_z] + order:
+        for p in x_others:
+            await_piece(p, z)
+            for d in range(1, y_side):
+                far = (at_y + d) % y_side * x_side + at_x
+                send(p, z, 0, (region, at_z * plane + far))
+        for p in y_others:
+            await_piece(p, z)
+            for d in range(1, x_side):
+                far = at_y * x_side + (at_x + d) % x_side
+                send(p, z, 1, (region, at_z * plane + far))
+    for p in x_others + y_others:
+        absorb(p)
+    for dy in range(1, y_side):
+        for dx in range(1, x_side):
+            far = (at_y + dy) % y_side * x_side + (at_x + dx) % x_side
+            for z in range(z_side):
+                await_piece(far, z, 0)
+                await_piece(far, z, 1)
+            absorb(far)
+    for copy in crossing + started:
+        copy.wait_send()
+
+
+def gathered_sums(ens_obs, obs_values, obs_var, edge_up, edge_down, loc_local, loc_edge):
+    regions, tiles = lax.axis_size("region"), lax.axis_size("tile")
+    records, members = ens_obs.shape
+    boxes, edges = loc_local.shape[0], edge_up.shape[0]
+    sides = 1 if regions == 2 else 2
+    rows = records + sides * edges
+    block_rows = rows + INFO_ROWS
+    z_side, y_side, x_side = tile_sides(tiles)
+    plane = y_side * x_side
+    sends = z_side - 1 + z_side * (x_side + y_side - 2) + 2 * z_side * (x_side - 1) * (y_side - 1)
+    return pl.pallas_call(
+        functools.partial(gather_kernel, regions, tiles),
+        out_shape=(
+            jax.ShapeDtypeStruct((boxes, members, members), jnp.float32),
+            jax.ShapeDtypeStruct((boxes, members), jnp.float32),
+        ),
+        in_specs=[pl.BlockSpec(memory_space=pltpu.VMEM)] * 7,
+        out_specs=[pl.BlockSpec(memory_space=pltpu.VMEM)] * 2,
+        scratch_shapes=[
+            pltpu.VMEM((plane, z_side, block_rows, members), jnp.bfloat16),
+            pltpu.VMEM((tiles, boxes, (rows + 127) // 128 * 128), jnp.float32),
+            pltpu.VMEM((sides, edges + INFO_ROWS, members), jnp.bfloat16),
+            pltpu.VMEM((sides, edges + INFO_ROWS, members), jnp.bfloat16),
+            pltpu.SemaphoreType.DMA((sends,)),
+            pltpu.SemaphoreType.DMA((2, plane, z_side)),
+            pltpu.SemaphoreType.DMA((sides,)),
+            pltpu.SemaphoreType.DMA((sides,)),
+        ],
+        compiler_params=pltpu.CompilerParams(
+            collective_id=0, has_side_effects=True, vmem_limit_bytes=48 * 1024 * 1024
+        ),
+        name="gather_gram",
+    )(ens_obs, obs_values.reshape(1, -1), obs_var.reshape(1, -1), edge_up.reshape(1, -1),
+      edge_down.reshape(1, -1), loc_local, loc_edge)
 
 
 def split(x):
@@ -128,36 +330,8 @@
 
 
 def body(ens_obs, obs_values, obs_var, edge_up, edge_down, loc_local, loc_edge, states, box_ids):
-    record_count = ens_obs.shape[0]
-    members = ens_obs.shape[1]
-    ymean = jnp.mean(ens_obs, axis=1, dtype=jnp.float32)
-    anomaly = (ens_obs.astype(jnp.float32) - ymean[:, None]).astype(jnp.bfloat16)
-    obs_info = jnp.stack([1.0 / obs_var, obs_values - ymean], axis=1).astype(jnp.bfloat16)
-    lower_a, lower_i = passed_along((anomaly[edge_up], obs_info[edge_up]), "region", 1)
-    upper_a, upper_i = passed_along((anomaly[edge_down], obs_info[edge_down]), "region", -1)
-    edge_anom = jnp.concatenate([lower_a, upper_a], axis=0)
-    edge_info = jnp.concatenate([lower_i, upper_i], axis=0)
-    block_anom = jnp.concatenate([anomaly, edge_anom], axis=0)
-    block_info = jnp.concatenate([obs_info, edge_info], axis=0)
-    all_anom, all_info = (
-        lax.all_gather(block_anom, "tile", axis=0, tiled=True),
-        lax.all_gather(block_info, "tile", axis=0, tiled=True),
-    )
-    tile_count = lax.axis_size("tile")
-    pool_rows = block_anom.shape[0]
-    all_anom = all_anom.reshape(tile_count, pool_rows, members)
-    all_info = all_info.reshape(tile_count, pool_rows, 2)
-    gram_one, innov_one = obs_terms(
-        all_anom[:, :record_count].reshape(-1, members),
-        all_info[:, :record_count].reshape(-1, 2),
-        loc_local,
-    )
-    gram_two, innov_two = obs_terms(
-        all_anom[:, record_count:].reshape(-1, members),
-        all_info[:, record_count:].reshape(-1, 2),
-        loc_edge,
-    )
-    return analyse(gram_one + gram_two, innov_one + innov_two, states, box_ids)
+    gram, innov = gathered_sums(ens_obs, obs_values, obs_var, edge_up, edge_down, loc_local, loc_edge)
+    return analyse(gram, innov, states, box_ids)
 
 
 def solution(mesh):

time: 142 us -> 71.7 us (0.50)
  the two profiles are of different devices: /device:TPU:2 before, /device:TPU:25 now
where the time goes in v2:
time: 71.7 us; the launch traced here: 71.3 us
  Pallas kernels  64.6 us (90%)
  local copies, waits for them, and re-layouts  6.65 us (9%)
    pallas_call x1, Pallas kernels, gathered_sums(): pl.pallas_call(functools.partial(gather_kernel, regions, tiles), out_shap...  39.9 us
    pallas_call x1, Pallas kernels, analyse(): pl.pallas_call(analyse_kernel, out_shape=jax.ShapeDtypeStruct(states.shap...  24.7 us
    unnamed x18, local copies, waits for them, and re-layouts  6.65 us

profile of v2, /device:TPU:25, one launch (start us, length us, event | category | flops | bytes accessed | tf_op | source)
XLA Modules:
  0.0 71.3 jit_solution(4794195159067461132)
XLA Ops:
  0.0 0.0 copy-start.1
  0.0 0.9 %copy-done.1 = bf16[128,512]{1,0:T(8,128)(2,1)S(1)} copy-done((bf16[128,512]{1,0:T(8,128)(2,1)S(1)}, bf16[128,512]{1,0:T(8,128)(2,1)}, u32[]{:S(2)}) %copy-start.1) | copy-done | bytes 131096
  0.9 0.0 copy-start.2
  0.9 0.7 %copy-done.2 = f32[2,2048]{1,0:T(2,128)S(1)} copy-done((f32[2,2048]{1,0:T(2,128)S(1)}, f32[2,2048]{1,0:T(2,128)}, u32[]{:S(2)}) %copy-start.2) | copy-done | bytes 16408
  1.6 0.0 copy-start.3
  1.6 0.7 copy-done.3
  2.3 0.0 copy-start.5
  2.3 0.7 copy-done.5
  3.0 0.0 copy-start.6
  3.0 0.7 copy-done.6
  3.6 0.0 copy-start.7
  3.6 0.7 copy-done.7
  4.3 0.0 copy-start.8
  4.3 0.7 copy-done.8
  4.9 39.9 %gather_gram.1 = (f32[2,512,512]{2,1,0:T(8,128)S(1)}, f32[2,512]{1,0:T(2,128)S(1)}) custom-call(bf16[128,512]{1,0:T(8,128)(2,1)S(1)} %copy-done.1, f32[1,128]{1,0:T(1,128)S(1)} %bitcast.6, f32[1,128]{1,0:T(1,128)S(1)} %bitcast.7, s32[1,32]{1,0:T(1,128)S(1)} %bitcast.8, s32[1,32]{1,0:T(1,128)S(1)} %bitcast.9, f32[2,2048]{1,0:T(2,128)S(1)} %copy-done.2, ...), custom_call_target="tpu_custom_call" | custom-call | tf_op jit(solution)/shard_map/gather_gram/pallas_call | solution.py:200
  44.9 0.0 copy-start
  44.9 1.0 %copy-done = bf16[2,256,512]{2,1,0:T(8,128)(2,1)S(1)} copy-done((bf16[2,256,512]{2,1,0:T(8,128)(2,1)S(1)}, bf16[2,256,512]{2,1,0:T(8,128)(2,1)}, u32[]{:S(2)}) %copy-start) | copy-done | bytes 524312
  45.9 0.0 copy-start.4
  45.9 0.7 copy-done.4
  46.6 24.7 %analyse.1 = bf16[2,256,512]{2,1,0:T(8,128)(2,1)} custom-call(f32[2,512,512]{2,1,0:T(8,128)S(1)} %get-tuple-element.7.gram_ref, f32[2,512]{1,0:T(2,128)S(1)} %get-tuple-element.8.innov_ref, bf16[2,256,512]{2,1,0:T(8,128)(2,1)S(1)} %copy-done, s32[1,256]{1,0:T(1,128)S(1)} %bitcast.5), custom_call_target="tpu_custom_call" | custom-call | tf_op jit(solution)/shard_map/analyse/pallas_call | solution.py:318
Async XLA Ops:
  0.0 0.9 %copy-start.1 = (bf16[128,512]{1,0:T(8,128)(2,1)S(1)}, bf16[128,512]{1,0:T(8,128)(2,1)}, u32[]{:S(2)}) copy-start(bf16[128,512]{1,0:T(8,128)(2,1)} %ens_ref.1) | copy-start | bytes 393220
  0.9 0.7 %copy-start.2 = (f32[2,2048]{1,0:T(2,128)S(1)}, f32[2,2048]{1,0:T(2,128)}, u32[]{:S(2)}) copy-start(f32[2,2048]{1,0:T(2,128)} %local_ref.1) | copy-start | bytes 49156
  1.6 0.7 copy-start.3
  2.3 0.7 copy-start.5
  3.0 0.7 copy-start.6
  3.6 0.7 copy-start.7
  4.3 0.7 copy-start.8
  44.9 1.0 %copy-start = (bf16[2,256,512]{2,1,0:T(8,128)(2,1)S(1)}, bf16[2,256,512]{2,1,0:T(8,128)(2,1)}, u32[]{:S(2)}) copy-start(bf16[2,256,512]{2,1,0:T(8,128)(2,1)} %states_ref.1) | copy-start | bytes 1572868
  45.9 0.7 copy-start.4

commit v3 on v2

--- a/solution.py
+++ b/solution.py
@@ -14,11 +14,19 @@
     return 4, 2, tiles // 8
 
 
-def gather_kernel(regions, tiles, ens_ref, values_ref, var_ref, up_ref, down_ref, local_ref, edge_ref,
-                  gram_ref, innov_ref, pool, weights, leaving, arriving,
+def gather_kernel(regions, tiles, ens_hbm, values_hbm, var_hbm, up_hbm, down_hbm, local_hbm, edge_hbm,
+                  gram_ref, innov_ref, ens_ref, values_ref, var_ref, up_ref, down_ref, local_ref, edge_ref,
+                  copy_sem, pool, weights, leaving, arriving,
                   send_sem, recv_sem, edge_send_sem, edge_recv_sem):
     region = lax.axis_index("region")
     tile = lax.axis_index("tile")
+    fetched = []
+    for number, (far, near) in enumerate([
+        (ens_hbm, ens_ref), (values_hbm, values_ref), (var_hbm, var_ref), (up_hbm, up_ref),
+        (down_hbm, down_ref), (local_hbm, local_ref), (edge_hbm, edge_ref),
+    ]):
+        fetched.append(pltpu.make_async_copy(far, near, copy_sem.at[number]))
+        fetched[-1].start()
     z_side, y_side, x_side = tile_sides(tiles)
     plane = y_side * x_side
     at_z, at_y, at_x = tile // plane, (tile // x_side) % y_side, tile % x_side
@@ -46,6 +54,8 @@
     for device in greeted:
         pl.semaphore_signal(barrier, inc=1, device_id=device, device_id_type=pl.DeviceIdType.MESH)
 
+    for copy in fetched[:5]:
+        copy.wait()
     wide = ens_ref[...].astype(jnp.float32)
     ymean = jnp.sum(wide, axis=1, keepdims=True) * (1.0 / members)
     anomaly = (wide - ymean).astype(jnp.bfloat16)
@@ -128,6 +138,8 @@
         send(at, at_z, None, (region, z * plane + at))
     spread(at_z)
 
+    for copy in fetched[5:]:
+        copy.wait()
     edge_columns = 2 * edges
     for t in range(tiles):
         weights[t, :, :records] = local_ref[:, t * records:(t + 1) * records]
@@ -197,15 +209,18 @@
     z_side, y_side, x_side = tile_sides(tiles)
     plane = y_side * x_side
     sends = z_side - 1 + z_side * (x_side + y_side - 2) + 2 * z_side * (x_side - 1) * (y_side - 1)
+    arrays = (ens_obs, obs_values.reshape(1, -1), obs_var.reshape(1, -1), edge_up.reshape(1, -1),
+              edge_down.reshape(1, -1), loc_local, loc_edge)
     return pl.pallas_call(
         functools.partial(gather_kernel, regions, tiles),
         out_shape=(
             jax.ShapeDtypeStruct((boxes, members, members), jnp.float32),
             jax.ShapeDtypeStruct((boxes, members), jnp.float32),
         ),
-        in_specs=[pl.BlockSpec(memory_space=pltpu.VMEM)] * 7,
+        in_specs=[pl.BlockSpec(memory_space=pl.ANY)] * 7,
         out_specs=[pl.BlockSpec(memory_space=pltpu.VMEM)] * 2,
-        scratch_shapes=[
+        scratch_shapes=[pltpu.VMEM(array.shape, array.dtype) for array in arrays] + [
+            pltpu.SemaphoreType.DMA((len(arrays),)),
             pltpu.VMEM((plane, z_side, block_rows, members), jnp.bfloat16),
             pltpu.VMEM((tiles, boxes, (rows + 127) // 128 * 128), jnp.float32),
             pltpu.VMEM((sides, edges + INFO_ROWS, members), jnp.bfloat16),
@@ -216,20 +231,15 @@
             pltpu.SemaphoreType.DMA((sides,)),
         ],
         compiler_params=pltpu.CompilerParams(
-            collective_id=0, has_side_effects=True, vmem_limit_bytes=48 * 1024 * 1024
+            collective_id=0, has_side_effects=True, vmem_limit_bytes=56 * 1024 * 1024
         ),
         name="gather_gram",
-    )(ens_obs, obs_values.reshape(1, -1), obs_var.reshape(1, -1), edge_up.reshape(1, -1),
-      edge_down.reshape(1, -1), loc_local, loc_edge)
+    )(*arrays)
 
 
 def split(x):
     high = x.astype(jnp.bfloat16)
     return high, (x - high.astype(jnp.float32)).astype(jnp.bfloat16)
-
-
-def dot_once(left, right):
-    return jnp.dot(left.astype(jnp.bfloat16), right.astype(jnp.bfloat16), preferred_element_type=jnp.float32)
 
 
 def dot_thrice(left, right):
@@ -248,7 +258,12 @@
     return error * error / (2.0 - error * error)
 
 
-def analyse_kernel(gram_ref, innov_ref, states_ref, ids_ref, out_ref, system, guess):
+def analyse_kernel(gram_ref, innov_ref, states_hbm, ids_hbm, out_ref, system_high, system_low, guess, answer,
+                   states_ref, ids_ref, copy_sem):
+    states_copy = pltpu.make_async_copy(states_hbm, states_ref, copy_sem.at[0])
+    ids_copy = pltpu.make_async_copy(ids_hbm, ids_ref, copy_sem.at[1])
+    states_copy.start()
+    ids_copy.start()
     boxes, members, _ = gram_ref.shape
     fields, cells, _ = states_ref.shape
     rows = lax.broadcasted_iota(jnp.int32, (members, members), 0)
@@ -264,10 +279,26 @@
         first = 2.0 / (top + ridge)
         error = (top - ridge) / (top + ridge)
         mu = 2.0 / (2.0 - error * error)
-        system[b] = full
-        guess[b] = (mu * first) * (2.0 * identity - first * full)
+        high, low = split(full)
+        system_high[b] = high
+        system_low[b] = low
+        start = (mu * first) * (2.0 * identity - first * full)
+        guess[b] = start.astype(jnp.bfloat16)
+        answer[b] = start
         errors.append(shrink(error))
         worst = jnp.maximum(worst, top / ridge)
+
+    def coarse(carried):
+        after = []
+        for b in range(boxes):
+            error = carried[b]
+            mu = 2.0 / (2.0 - error * error)
+            held = guess[b]
+            left = identity - jnp.dot(system_high[b], held, preferred_element_type=jnp.float32)
+            more = jnp.dot(held, left.astype(jnp.bfloat16), preferred_element_type=jnp.float32)
+            guess[b] = (mu * (held.astype(jnp.float32) + more)).astype(jnp.bfloat16)
+            after.append(shrink(error))
+        return tuple(after)
 
     def refine(dot):
         def step(carried):
@@ -275,27 +306,44 @@
             for b in range(boxes):
                 error = carried[b]
                 mu = 2.0 / (2.0 - error * error)
-                left = 2.0 * identity - dot(system[b], guess[b])
-                guess[b] = mu * dot(guess[b], left)
+                full = gram_ref[b] + ridge * identity
+                left = 2.0 * identity - dot(full, answer[b])
+                answer[b] = mu * dot(answer[b], left)
                 after.append(shrink(error))
             return tuple(after)
         return step
 
-    def above(limit, allowed):
+    def above(limit):
         def proceed(carried):
             top = carried[0]
             for error in carried[1:]:
                 top = jnp.maximum(top, error)
-            return jnp.logical_and(allowed, top > limit)
+            return top > limit
         return proceed
 
     easy = worst < 64.0
     hard = worst > 2048.0
-    errors = lax.while_loop(above(0.005, easy), refine(dot_once), tuple(errors))
-    errors = tuple(jnp.maximum(error, 0.02) for error in errors)
-    errors = lax.while_loop(above(3e-4, jnp.logical_not(hard)), refine(dot_thrice), errors)
-    errors = lax.while_loop(above(1e-6, hard), refine(dot_full), errors)
-
+
+    @pl.when(easy)
+    def _():
+        lax.while_loop(above(0.005), coarse, tuple(errors))
+        for b in range(boxes):
+            held = guess[b]
+            left = identity - jnp.dot(system_high[b], held, preferred_element_type=jnp.float32)
+            left = left - jnp.dot(system_low[b], held, preferred_element_type=jnp.float32)
+            more = jnp.dot(held, left.astype(jnp.bfloat16), preferred_element_type=jnp.float32)
+            answer[b] = held.astype(jnp.float32) + more
+
+    @pl.when(jnp.logical_and(jnp.logical_not(easy), jnp.logical_not(hard)))
+    def _():
+        lax.while_loop(above(3e-4), refine(dot_thrice), tuple(errors))
+
+    @pl.when(hard)
+    def _():
+        lax.while_loop(above(1e-6), refine(dot_full), tuple(errors))
+
+    states_copy.wait()
+    ids_copy.wait()
     wide = states_ref[...].astype(jnp.float32).reshape(fields * cells, members)
     smean = jnp.sum(wide, axis=1, keepdims=True) * (1.0 / members)
     anomaly = (wide - smean).astype(jnp.bfloat16)
@@ -305,7 +353,7 @@
     ids = jnp.concatenate([ids] * fields, axis=0)
     total = jnp.zeros((fields * cells, members), jnp.float32)
     for b in range(boxes):
-        inverse = guess[b]
+        inverse = answer[b]
         wbar = jnp.sum(inverse * innov_ref[b:b + 1, :], axis=1, keepdims=True)
         transform = (0.5 * identity + (0.5 * ridge) * inverse + wbar).astype(jnp.bfloat16)
         update = jnp.dot(anomaly, transform, preferred_element_type=jnp.float32)
@@ -315,16 +363,22 @@
 
 def analyse(gram, innov, states, box_ids):
     boxes, members, _ = gram.shape
+    square = (boxes, members, members)
     return pl.pallas_call(
         analyse_kernel,
         out_shape=jax.ShapeDtypeStruct(states.shape, jnp.bfloat16),
-        in_specs=[pl.BlockSpec(memory_space=pltpu.VMEM)] * 4,
+        in_specs=[pl.BlockSpec(memory_space=pltpu.VMEM)] * 2 + [pl.BlockSpec(memory_space=pl.ANY)] * 2,
         out_specs=pl.BlockSpec(memory_space=pltpu.VMEM),
         scratch_shapes=[
-            pltpu.VMEM((boxes, members, members), jnp.float32),
-            pltpu.VMEM((boxes, members, members), jnp.float32),
+            pltpu.VMEM(square, jnp.bfloat16),
+            pltpu.VMEM(square, jnp.bfloat16),
+            pltpu.VMEM(square, jnp.bfloat16),
+            pltpu.VMEM(square, jnp.float32),
+            pltpu.VMEM(states.shape, jnp.bfloat16),
+            pltpu.VMEM((1, box_ids.shape[0]), jnp.int32),
+            pltpu.SemaphoreType.DMA((2,)),
         ],
-        compiler_params=pltpu.CompilerParams(vmem_limit_bytes=48 * 1024 * 1024),
+        compiler_params=pltpu.CompilerParams(vmem_limit_bytes=56 * 1024 * 1024),
         name="analyse",
     )(gram, innov, states, box_ids.reshape(1, -1))
 

time: 71.7 us -> 68.9 us (0.961)
  the two profiles are of different devices: /device:TPU:25 before, /device:TPU:24 now
where the time goes in v3:
time: 68.9 us; the launch traced here: 68.7 us
  Pallas kernels  68.5 us (99%)
    pallas_call x1, Pallas kernels, gathered_sums(): pl.pallas_call(functools.partial(gather_kernel, regions, tiles), out_shap...  41.6 us
    pallas_call x1, Pallas kernels, analyse(): pl.pallas_call(analyse_kernel, out_shape=jax.ShapeDtypeStruct(states.shap...  26.9 us

profile of v3, /device:TPU:24, one launch (start us, length us, event | category | flops | bytes accessed | tf_op | source)
XLA Modules:
  0.0 68.7 jit_solution(9067418062966430912)
XLA Ops:
  0.0 41.6 %gather_gram.1 = (f32[2,512,512]{2,1,0:T(8,128)}, f32[2,512]{1,0:T(2,128)}) custom-call(bf16[128,512]{1,0:T(8,128)(2,1)} %ens_hbm.1, f32[1,128]{1,0:T(1,128)} %bitcast.6, f32[1,128]{1,0:T(1,128)} %bitcast.7, s32[1,32]{1,0:T(1,128)} %bitcast.8, s32[1,32]{1,0:T(1,128)} %bitcast.9, f32[2,2048]{1,0:T(2,128)} %local_hbm.1, f32[2,1024]{1,0:T(2,128)} %edge_hbm.1), custom_call_target="tpu_custom_call" | custom-call | tf_op jit(solution)/shard_map/gather_gram/pallas_call | solution.py:214
  41.6 26.9 %analyse.1 = bf16[2,256,512]{2,1,0:T(8,128)(2,1)} custom-call(f32[2,512,512]{2,1,0:T(8,128)} %get-tuple-element.7.gram_ref, f32[2,512]{1,0:T(2,128)} %get-tuple-element.8.innov_ref, bf16[2,256,512]{2,1,0:T(8,128)(2,1)} %states_hbm.1, s32[1,256]{1,0:T(1,128)} %bitcast.5), custom_call_target="tpu_custom_call" | custom-call | tf_op jit(solution)/shard_map/analyse/pallas_call | solution.py:367

commit v4 on v3

--- a/solution.py
+++ b/solution.py
@@ -8,6 +8,7 @@
 
 
 INFO_ROWS = 16
+LANES = 128
 
 
 def tile_sides(tiles):
@@ -16,7 +17,7 @@
 
 def gather_kernel(regions, tiles, ens_hbm, values_hbm, var_hbm, up_hbm, down_hbm, local_hbm, edge_hbm,
                   gram_ref, innov_ref, ens_ref, values_ref, var_ref, up_ref, down_ref, local_ref, edge_ref,
-                  copy_sem, pool, weights, leaving, arriving,
+                  copy_sem, pool, near_weights, far_weights, leaving, arriving,
                   send_sem, recv_sem, edge_send_sem, edge_recv_sem):
     region = lax.axis_index("region")
     tile = lax.axis_index("tile")
@@ -35,22 +36,23 @@
     boxes = local_ref.shape[0]
     edges = up_ref.shape[1]
     sides = leaving.shape[0]
-    rows = records + sides * edges
     block_rows = pool.shape[2]
+    info_at = block_rows - INFO_ROWS
+    parts = members // LANES
     cut = (block_rows // 2 + 15) // 16 * 16
 
     x_others = [at_y * x_side + (at_x + d) % x_side for d in range(1, x_side)]
     y_others = [(at_y + d) % y_side * x_side + at_x for d in range(1, y_side)]
     z_others = [(at_z + d) % z_side for d in range(1, z_side)]
     if sides == 1:
-        partners = [(1 - region, 0)]
+        partners = [1 - region]
     else:
-        partners = [((region + 1) % regions, 0), ((region + regions - 1) % regions, 1)]
+        partners = [(region + 1) % regions, (region + regions - 1) % regions]
 
     barrier = pltpu.get_barrier_semaphore()
     greeted = [(region, z * plane + at) for z in z_others]
     greeted += [(region, at_z * plane + p) for p in x_others + y_others]
-    greeted += [(partner, tile) for partner, _ in partners]
+    greeted += [(partner, tile) for partner in partners]
     for device in greeted:
         pl.semaphore_signal(barrier, inc=1, device_id=device, device_id_type=pl.DeviceIdType.MESH)
 
@@ -62,51 +64,17 @@
     row_at = lax.broadcasted_iota(jnp.int32, (records, records), 0)
     column_at = lax.broadcasted_iota(jnp.int32, (records, records), 1)
     ymean_row = jnp.sum(jnp.where(row_at == column_at, ymean, 0.0), axis=0, keepdims=True)
+    index_row = jnp.concatenate(
+        [up_ref[...].astype(jnp.float32), down_ref[...].astype(jnp.float32),
+         jnp.zeros((1, LANES - 2 * edges), jnp.float32)], axis=1)
     info = jnp.concatenate(
-        [1.0 / var_ref[...], values_ref[...] - ymean_row, jnp.zeros((INFO_ROWS - 2, records), jnp.float32)], axis=0
-    ).astype(jnp.bfloat16)
-
-    def picked(index_row, keep):
-        index = jnp.concatenate([index_row] * (records // edges), axis=1)
-        chosen = jnp.where(row_at == index, keep, 0.0)
-        far_info = jnp.dot(info, chosen.astype(jnp.bfloat16), preferred_element_type=jnp.float32)
-        chosen = chosen.T[:edges].astype(jnp.bfloat16)
-        far = jnp.dot(chosen, anomaly, preferred_element_type=jnp.float32)
-        return far.astype(jnp.bfloat16), far_info.astype(jnp.bfloat16)
-
-    if sides == 1:
-        chosen_row = jnp.where(region == 0, up_ref[...], down_ref[...])
-        going = [picked(chosen_row, 1.0)]
-    else:
-        going = [
-            picked(up_ref[...], jnp.where(region == regions - 1, 0.0, 1.0)),
-            picked(down_ref[...], jnp.where(region == 0, 0.0, 1.0)),
-        ]
-    for side, (far, far_info) in enumerate(going):
-        leaving[side, :edges, :] = far
-        leaving[side, edges:, :records] = far_info
-        leaving[side, edges:, records:] = jnp.zeros((INFO_ROWS, members - records), jnp.bfloat16)
-    pool[at, at_z, :records, :] = anomaly
-
+        [1.0 / var_ref[...], values_ref[...] - ymean_row, index_row,
+         jnp.zeros((INFO_ROWS - 3, records), jnp.float32)], axis=0)
+    for part in range(parts):
+        pool[at, at_z, part * records:(part + 1) * records, :] = anomaly[:, part * LANES:(part + 1) * LANES]
+    pool[at, at_z, info_at:, :] = info.astype(jnp.bfloat16)
     pl.semaphore_wait(barrier, len(greeted))
     started = []
-    crossing = []
-    for partner, side in partners:
-        copy = pltpu.make_async_remote_copy(
-            src_ref=leaving.at[side], dst_ref=arriving.at[side],
-            send_sem=edge_send_sem.at[side], recv_sem=edge_recv_sem.at[side],
-            device_id=(partner, tile), device_id_type=pl.DeviceIdType.MESH,
-        )
-        copy.start()
-        crossing.append(copy)
-    for copy in crossing:
-        copy.wait_recv()
-    pieces = [info]
-    for side in range(sides):
-        pool[at, at_z, pl.ds(records + side * edges, edges), :] = arriving[side, :edges, :]
-        pieces.append(arriving[side, edges:, :edges])
-    pieces.append(jnp.zeros((INFO_ROWS, members - rows), jnp.bfloat16))
-    pool[at, at_z, rows:, :] = jnp.concatenate(pieces, axis=1)
 
     def piece(place, z, part):
         if part is None:
@@ -140,29 +108,25 @@
 
     for copy in fetched[5:]:
         copy.wait()
-    edge_columns = 2 * edges
     for t in range(tiles):
-        weights[t, :, :records] = local_ref[:, t * records:(t + 1) * records]
-        near = edge_ref[:, t * edge_columns:(t + 1) * edge_columns]
+        near_weights[t] = local_ref[:, t * records:(t + 1) * records]
+    for place in range(plane):
+        columns = [(z * plane + place) * 2 * edges for z in range(z_side)]
+        lower = jnp.concatenate([edge_ref[:, c:c + edges] for c in columns], axis=1)
+        upper = jnp.concatenate([edge_ref[:, c + edges:c + 2 * edges] for c in columns], axis=1)
         if sides == 1:
-            near = jnp.where(region == 0, near[:, edges:], near[:, :edges])
-        weights[t, :, records:rows] = near
-
-    def absorb(place, first=False):
-        block = pool[place]
-        data = jnp.concatenate(
-            [block[:, :records].reshape(z_side * records, members),
-             block[:, records:rows].reshape(z_side * (rows - records), members)], axis=0)
+            far_weights[0, place] = jnp.where(region == 0, upper, lower)
+        else:
+            far_weights[0, place] = lower
+            far_weights[1, place] = upper
+
+    def flat(block):
+        return jnp.concatenate([block[part * records:(part + 1) * records] for part in range(parts)], axis=1)
+
+    def add(data, inverse_var, innovation, loc, first=False):
+        scale = loc * inverse_var
+        weighted = (scale * innovation).astype(jnp.bfloat16)
         turned = data.astype(jnp.float32).T
-        inverse_var = [block[z, rows:, :rows].astype(jnp.float32)[0:1] for z in range(z_side)]
-        innovation = [block[z, rows:, :rows].astype(jnp.float32)[1:2] for z in range(z_side)]
-        loc = [weights[z * plane + place][:, :rows] for z in range(z_side)]
-
-        def ordered(parts):
-            return jnp.concatenate([p[:, :records] for p in parts] + [p[:, records:] for p in parts], axis=1)
-
-        scale = ordered(loc) * ordered(inverse_var)
-        weighted = (scale * ordered(innovation)).astype(jnp.bfloat16)
         more = jnp.dot(weighted, data, preferred_element_type=jnp.float32)
         innov_ref[...] = more if first else innov_ref[...] + more
         for b in range(boxes):
@@ -170,11 +134,60 @@
             more = jnp.dot(scaled, data, preferred_element_type=jnp.float32)
             gram_ref[b] = more if first else gram_ref[b] + more
 
+    def crossing(place, side):
+        return pltpu.make_async_remote_copy(
+            src_ref=leaving.at[side, place], dst_ref=arriving.at[side, place],
+            send_sem=edge_send_sem.at[side, place], recv_sem=edge_recv_sem.at[side, place],
+            device_id=(partners[side], tile), device_id_type=pl.DeviceIdType.MESH,
+        )
+
+    def near_group(place, first=False):
+        data = jnp.concatenate([flat(pool[place, z]) for z in range(z_side)], axis=0)
+        infos = [pool[place, z, info_at:, :] for z in range(z_side)]
+        info = jnp.concatenate(infos, axis=1)
+        wide_infos = [each.astype(jnp.float32) for each in infos]
+        for side in range(sides):
+            if sides == 1:
+                index = [jnp.where(region == 0, each[2:3, :edges], each[2:3, edges:2 * edges]) for each in wide_infos]
+                keep = 1.0
+            else:
+                index = [each[2:3, side * edges:(side + 1) * edges] for each in wide_infos]
+                keep = jnp.where(region == (0 if side else regions - 1), 0.0, 1.0)
+            index = jnp.concatenate([index[z] + float(z * records) for z in range(z_side)], axis=1)
+            picked = z_side * edges
+            row_of = lax.broadcasted_iota(jnp.int32, (z_side * records, picked), 0).astype(jnp.float32)
+            chosen = jnp.where(row_of == index, keep, 0.0)
+            far_info = jnp.dot(info, chosen.astype(jnp.bfloat16), preferred_element_type=jnp.float32)
+            far = jnp.dot(chosen.T.astype(jnp.bfloat16), data, preferred_element_type=jnp.float32)
+            far = far.astype(jnp.bfloat16)
+            for part in range(parts):
+                leaving[side, place, part * picked:(part + 1) * picked, :] = far[:, part * LANES:(part + 1) * LANES]
+            leaving[side, place, parts * picked:, :] = far_info.astype(jnp.bfloat16)
+            crossing(place, side).start()
+        wide_info = info.astype(jnp.float32)
+        loc = jnp.concatenate([near_weights[z * plane + place] for z in range(z_side)], axis=1)
+        return lambda: add(data, wide_info[0:1], wide_info[1:2], loc, first)
+
+    def far_groups(places):
+        data, info, loc = [], [], []
+        picked = z_side * edges
+        for place in places:
+            for side in range(sides):
+                crossing(place, side).wait_recv()
+                block = arriving[side, place]
+                data.append(jnp.concatenate(
+                    [block[part * picked:(part + 1) * picked] for part in range(parts)], axis=1))
+                info.append(block[parts * picked:].astype(jnp.float32))
+                loc.append(far_weights[side, place])
+        data = jnp.concatenate(data, axis=0)
+        info = jnp.concatenate(info, axis=1)
+        add(data, info[0:1], info[1:2], jnp.concatenate(loc, axis=1))
+
     order = [(at_z + z_side - d) % z_side for d in range(1, z_side)]
     for z in order:
         await_piece(at, z)
         spread(z)
-    absorb(at, first=True)
+    near_group(at, first=True)()
     for z in [at_z] + order:
         for p in x_others:
             await_piece(p, z)
@@ -187,15 +200,22 @@
                 far = at_y * x_side + (at_x + d) % x_side
                 send(p, z, 1, (region, at_z * plane + far))
     for p in x_others + y_others:
-        absorb(p)
-    for dy in range(1, y_side):
-        for dx in range(1, x_side):
-            far = (at_y + dy) % y_side * x_side + (at_x + dx) % x_side
-            for z in range(z_side):
-                await_piece(far, z, 0)
-                await_piece(far, z, 1)
-            absorb(far)
-    for copy in crossing + started:
+        near_group(p)()
+    far_groups([at] + x_others + y_others)
+    diagonal = [
+        (at_y + dy) % y_side * x_side + (at_x + dx) % x_side
+        for dy in range(1, y_side) for dx in range(1, x_side)
+    ]
+    for far in diagonal:
+        for z in [at_z] + order:
+            await_piece(far, z, 0)
+            await_piece(far, z, 1)
+        near_group(far)()
+    far_groups(diagonal)
+    for place in [at] + x_others + y_others + diagonal:
+        for side in range(sides):
+            crossing(place, side).wait_send()
+    for copy in started:
         copy.wait_send()
 
 
@@ -204,10 +224,10 @@
     records, members = ens_obs.shape
     boxes, edges = loc_local.shape[0], edge_up.shape[0]
     sides = 1 if regions == 2 else 2
-    rows = records + sides * edges
-    block_rows = rows + INFO_ROWS
     z_side, y_side, x_side = tile_sides(tiles)
     plane = y_side * x_side
+    block_rows = members // LANES * records + INFO_ROWS
+    edge_rows = members // LANES * z_side * edges + INFO_ROWS
     sends = z_side - 1 + z_side * (x_side + y_side - 2) + 2 * z_side * (x_side - 1) * (y_side - 1)
     arrays = (ens_obs, obs_values.reshape(1, -1), obs_var.reshape(1, -1), edge_up.reshape(1, -1),
               edge_down.reshape(1, -1), loc_local, loc_edge)
@@ -221,14 +241,15 @@
         out_specs=[pl.BlockSpec(memory_space=pltpu.VMEM)] * 2,
         scratch_shapes=[pltpu.VMEM(array.shape, array.dtype) for array in arrays] + [
             pltpu.SemaphoreType.DMA((len(arrays),)),
-            pltpu.VMEM((plane, z_side, block_rows, members), jnp.bfloat16),
-            pltpu.VMEM((tiles, boxes, (rows + 127) // 128 * 128), jnp.float32),
-            pltpu.VMEM((sides, edges + INFO_ROWS, members), jnp.bfloat16),
-            pltpu.VMEM((sides, edges + INFO_ROWS, members), jnp.bfloat16),
+            pltpu.VMEM((plane, z_side, block_rows, LANES), jnp.bfloat16),
+            pltpu.VMEM((tiles, boxes, records), jnp.float32),
+            pltpu.VMEM((sides, plane, boxes, z_side * edges), jnp.float32),
+            pltpu.VMEM((sides, plane, edge_rows, LANES), jnp.bfloat16),
+            pltpu.VMEM((sides, plane, edge_rows, LANES), jnp.bfloat16),
             pltpu.SemaphoreType.DMA((sends,)),
             pltpu.SemaphoreType.DMA((2, plane, z_side)),
-            pltpu.SemaphoreType.DMA((sides,)),
-            pltpu.SemaphoreType.DMA((sides,)),
+            pltpu.SemaphoreType.DMA((sides, plane)),
+            pltpu.SemaphoreType.DMA((sides, plane)),
         ],
         compiler_params=pltpu.CompilerParams(
             collective_id=0, has_side_effects=True, vmem_limit_bytes=56 * 1024 * 1024
@@ -326,7 +347,7 @@
 
     @pl.when(easy)
     def _():
-        lax.while_loop(above(0.005), coarse, tuple(errors))
+        lax.while_loop(above(0.02), coarse, tuple(errors))
         for b in range(boxes):
             held = guess[b]
             left = identity - jnp.dot(system_high[b], held, preferred_element_type=jnp.float32)

time: 68.9 us -> 59.7 us (0.87)
  the two profiles are of different devices: /device:TPU:24 before, /device:TPU:0 now
where the time goes in v4:
time: 59.7 us; the launch traced here: 59 us
  Pallas kernels  58.8 us (98%)
    pallas_call x1, Pallas kernels, gathered_sums(): pl.pallas_call(functools.partial(gather_kernel, regions, tiles), out_shap...  31.9 us
    pallas_call x1, Pallas kernels, analyse(): pl.pallas_call(analyse_kernel, out_shape=jax.ShapeDtypeStruct(states.shap...  26.9 us

profile of v4, /device:TPU:0, one launch (start us, length us, event | category | flops | bytes accessed | tf_op | source)
XLA Modules:
  0.0 59.0 jit_solution(17668852347883697190)
XLA Ops:
  0.0 31.9 %gather_gram.1 = (f32[2,512,512]{2,1,0:T(8,128)}, f32[2,512]{1,0:T(2,128)}) custom-call(bf16[128,512]{1,0:T(8,128)(2,1)} %ens_hbm.1, f32[1,128]{1,0:T(1,128)} %bitcast.6, f32[1,128]{1,0:T(1,128)} %bitcast.7, s32[1,32]{1,0:T(1,128)} %bitcast.8, s32[1,32]{1,0:T(1,128)} %bitcast.9, f32[2,2048]{1,0:T(2,128)} %local_hbm.1, f32[2,1024]{1,0:T(2,128)} %edge_hbm.1), custom_call_target="tpu_custom_call" | custom-call | tf_op jit(solution)/shard_map/gather_gram/pallas_call | solution.py:234
  31.9 26.9 %analyse.1 = bf16[2,256,512]{2,1,0:T(8,128)(2,1)} custom-call(f32[2,512,512]{2,1,0:T(8,128)} %get-tuple-element.7.gram_ref, f32[2,512]{1,0:T(2,128)} %get-tuple-element.8.innov_ref, bf16[2,256,512]{2,1,0:T(8,128)(2,1)} %states_hbm.1, s32[1,256]{1,0:T(1,128)} %bitcast.5), custom_call_target="tpu_custom_call" | custom-call | tf_op jit(solution)/shard_map/analyse/pallas_call | solution.py:388

commit v5 on v4

--- a/solution.py
+++ b/solution.py
@@ -9,6 +9,7 @@
 
 INFO_ROWS = 16
 LANES = 128
+UNIT = 4
 
 
 def tile_sides(tiles):
@@ -110,18 +111,16 @@
         copy.wait()
     for t in range(tiles):
         near_weights[t] = local_ref[:, t * records:(t + 1) * records]
-    for place in range(plane):
-        columns = [(z * plane + place) * 2 * edges for z in range(z_side)]
-        lower = jnp.concatenate([edge_ref[:, c:c + edges] for c in columns], axis=1)
-        upper = jnp.concatenate([edge_ref[:, c + edges:c + 2 * edges] for c in columns], axis=1)
+        lower = edge_ref[:, 2 * t * edges:(2 * t + 1) * edges]
+        upper = edge_ref[:, (2 * t + 1) * edges:(2 * t + 2) * edges]
         if sides == 1:
-            far_weights[0, place] = jnp.where(region == 0, upper, lower)
+            far_weights[0, t] = jnp.where(region == 0, upper, lower)
         else:
-            far_weights[0, place] = lower
-            far_weights[1, place] = upper
-
-    def flat(block):
-        return jnp.concatenate([block[part * records:(part + 1) * records] for part in range(parts)], axis=1)
+            far_weights[0, t] = lower
+            far_weights[1, t] = upper
+
+    def flat(block, count):
+        return jnp.concatenate([block[part * count:(part + 1) * count] for part in range(parts)], axis=1)
 
     def add(data, inverse_var, innovation, loc, first=False):
         scale = loc * inverse_var
@@ -134,51 +133,59 @@
             more = jnp.dot(scaled, data, preferred_element_type=jnp.float32)
             gram_ref[b] = more if first else gram_ref[b] + more
 
-    def crossing(place, side):
+    units = []
+
+    def crossing(unit, side):
+        extent = pl.ds(0, parts * len(units[unit]) * edges + INFO_ROWS)
         return pltpu.make_async_remote_copy(
-            src_ref=leaving.at[side, place], dst_ref=arriving.at[side, place],
-            send_sem=edge_send_sem.at[side, place], recv_sem=edge_recv_sem.at[side, place],
+            src_ref=leaving.at[side, unit, extent], dst_ref=arriving.at[side, unit, extent],
+            send_sem=edge_send_sem.at[side, unit], recv_sem=edge_recv_sem.at[side, unit],
             device_id=(partners[side], tile), device_id_type=pl.DeviceIdType.MESH,
         )
 
-    def near_group(place, first=False):
-        data = jnp.concatenate([flat(pool[place, z]) for z in range(z_side)], axis=0)
-        infos = [pool[place, z, info_at:, :] for z in range(z_side)]
+    def near_unit(blocks):
+        unit = len(units)
+        units.append(blocks)
+        data = jnp.concatenate([flat(pool[place, z], records) for place, z in blocks], axis=0)
+        infos = [pool[place, z, info_at:, :] for place, z in blocks]
         info = jnp.concatenate(infos, axis=1)
-        wide_infos = [each.astype(jnp.float32) for each in infos]
+        index_rows = [each.astype(jnp.float32)[2:3] for each in infos]
+        picked = len(blocks) * edges
         for side in range(sides):
             if sides == 1:
-                index = [jnp.where(region == 0, each[2:3, :edges], each[2:3, edges:2 * edges]) for each in wide_infos]
+                index = [jnp.where(region == 0, each[:, :edges], each[:, edges:2 * edges]) for each in index_rows]
                 keep = 1.0
             else:
-                index = [each[2:3, side * edges:(side + 1) * edges] for each in wide_infos]
+                index = [each[:, side * edges:(side + 1) * edges] for each in index_rows]
                 keep = jnp.where(region == (0 if side else regions - 1), 0.0, 1.0)
-            index = jnp.concatenate([index[z] + float(z * records) for z in range(z_side)], axis=1)
-            picked = z_side * edges
-            row_of = lax.broadcasted_iota(jnp.int32, (z_side * records, picked), 0).astype(jnp.float32)
+            index = jnp.concatenate([each + float(n * records) for n, each in enumerate(index)], axis=1)
+            index = jnp.concatenate([index, jnp.full((1, LANES - picked), -1.0, jnp.float32)], axis=1) if picked < LANES else index
+            row_of = lax.broadcasted_iota(jnp.int32, (len(blocks) * records, LANES), 0).astype(jnp.float32)
             chosen = jnp.where(row_of == index, keep, 0.0)
             far_info = jnp.dot(info, chosen.astype(jnp.bfloat16), preferred_element_type=jnp.float32)
-            far = jnp.dot(chosen.T.astype(jnp.bfloat16), data, preferred_element_type=jnp.float32)
+            far = jnp.dot(chosen.T[:picked].astype(jnp.bfloat16), data, preferred_element_type=jnp.float32)
             far = far.astype(jnp.bfloat16)
             for part in range(parts):
-                leaving[side, place, part * picked:(part + 1) * picked, :] = far[:, part * LANES:(part + 1) * LANES]
-            leaving[side, place, parts * picked:, :] = far_info.astype(jnp.bfloat16)
-            crossing(place, side).start()
+                leaving[side, unit, part * picked:(part + 1) * picked, :] = far[:, part * LANES:(part + 1) * LANES]
+            leaving[side, unit, parts * picked:parts * picked + INFO_ROWS, :] = far_info.astype(jnp.bfloat16)
+            crossing(unit, side).start()
         wide_info = info.astype(jnp.float32)
-        loc = jnp.concatenate([near_weights[z * plane + place] for z in range(z_side)], axis=1)
-        return lambda: add(data, wide_info[0:1], wide_info[1:2], loc, first)
-
-    def far_groups(places):
+        loc = jnp.concatenate([near_weights[z * plane + place] for place, z in blocks], axis=1)
+        add(data, wide_info[0:1], wide_info[1:2], loc, unit == 0)
+
+    def near_units(blocks):
+        for start in range(0, len(blocks), UNIT):
+            near_unit(blocks[start:start + UNIT])
+
+    def far_units(first, last):
         data, info, loc = [], [], []
-        picked = z_side * edges
-        for place in places:
+        for unit in range(first, last):
+            picked = len(units[unit]) * edges
             for side in range(sides):
-                crossing(place, side).wait_recv()
-                block = arriving[side, place]
-                data.append(jnp.concatenate(
-                    [block[part * picked:(part + 1) * picked] for part in range(parts)], axis=1))
-                info.append(block[parts * picked:].astype(jnp.float32))
-                loc.append(far_weights[side, place])
+                crossing(unit, side).wait_recv()
+                data.append(flat(arriving[side, unit, :parts * picked, :], picked))
+                info.append(arriving[side, unit, parts * picked:parts * picked + INFO_ROWS, :].astype(jnp.float32)[:, :picked])
+                loc += [far_weights[side, z * plane + place] for place, z in units[unit]]
         data = jnp.concatenate(data, axis=0)
         info = jnp.concatenate(info, axis=1)
         add(data, info[0:1], info[1:2], jnp.concatenate(loc, axis=1))
@@ -187,8 +194,9 @@
     for z in order:
         await_piece(at, z)
         spread(z)
-    near_group(at, first=True)()
-    for z in [at_z] + order:
+    order = [at_z] + order
+    near_units([(at, z) for z in order])
+    for z in order:
         for p in x_others:
             await_piece(p, z)
             for d in range(1, y_side):
@@ -199,22 +207,23 @@
             for d in range(1, x_side):
                 far = at_y * x_side + (at_x + d) % x_side
                 send(p, z, 1, (region, at_z * plane + far))
-    for p in x_others + y_others:
-        near_group(p)()
-    far_groups([at] + x_others + y_others)
+        near_units([(p, z) for p in x_others + y_others])
+    early = len(units)
+    far_units(0, early)
     diagonal = [
         (at_y + dy) % y_side * x_side + (at_x + dx) % x_side
         for dy in range(1, y_side) for dx in range(1, x_side)
     ]
-    for far in diagonal:
-        for z in [at_z] + order:
+    for start in range(0, z_side, 2):
+        blocks = [(far, z) for far in diagonal for z in order[start:start + 2]]
+        for far, z in blocks:
             await_piece(far, z, 0)
             await_piece(far, z, 1)
-        near_group(far)()
-    far_groups(diagonal)
-    for place in [at] + x_others + y_others + diagonal:
+        near_units(blocks)
+    far_units(early, len(units))
+    for unit in range(len(units)):
         for side in range(sides):
-            crossing(place, side).wait_send()
+            crossing(unit, side).wait_send()
     for copy in started:
         copy.wait_send()
 
@@ -227,7 +236,10 @@
     z_side, y_side, x_side = tile_sides(tiles)
     plane = y_side * x_side
     block_rows = members // LANES * records + INFO_ROWS
-    edge_rows = members // LANES * z_side * edges + INFO_ROWS
+    edge_rows = members // LANES * UNIT * edges + INFO_ROWS
+    sideways = x_side + y_side - 2
+    corners = (x_side - 1) * (y_side - 1)
+    units = 1 + z_side * (-(-sideways // UNIT)) + z_side // 2 * (-(-2 * corners // UNIT))
     sends = z_side - 1 + z_side * (x_side + y_side - 2) + 2 * z_side * (x_side - 1) * (y_side - 1)
     arrays = (ens_obs, obs_values.reshape(1, -1), obs_var.reshape(1, -1), edge_up.reshape(1, -1),
               edge_down.reshape(1, -1), loc_local, loc_edge)
@@ -243,13 +255,13 @@
             pltpu.SemaphoreType.DMA((len(arrays),)),
             pltpu.VMEM((plane, z_side, block_rows, LANES), jnp.bfloat16),
             pltpu.VMEM((tiles, boxes, records), jnp.float32),
-            pltpu.VMEM((sides, plane, boxes, z_side * edges), jnp.float32),
-            pltpu.VMEM((sides, plane, edge_rows, LANES), jnp.bfloat16),
-            pltpu.VMEM((sides, plane, edge_rows, LANES), jnp.bfloat16),
+            pltpu.VMEM((sides, tiles, boxes, edges), jnp.float32),
+            pltpu.VMEM((sides, units, edge_rows, LANES), jnp.bfloat16),
+            pltpu.VMEM((sides, units, edge_rows, LANES), jnp.bfloat16),
             pltpu.SemaphoreType.DMA((sends,)),
             pltpu.SemaphoreType.DMA((2, plane, z_side)),
-            pltpu.SemaphoreType.DMA((sides, plane)),
-            pltpu.SemaphoreType.DMA((sides, plane)),
+            pltpu.SemaphoreType.DMA((sides, units)),
+            pltpu.SemaphoreType.DMA((sides, units)),
         ],
         compiler_params=pltpu.CompilerParams(
             collective_id=0, has_side_effects=True, vmem_limit_bytes=56 * 1024 * 1024
@@ -279,12 +291,17 @@
     return error * error / (2.0 - error * error)
 
 
-def analyse_kernel(gram_ref, innov_ref, states_hbm, ids_hbm, out_ref, system_high, system_low, guess, answer,
-                   states_ref, ids_ref, copy_sem):
+def analyse_kernel(gram_hbm, innov_ref, states_hbm, ids_hbm, out_ref, system_high, system_low, guess, answer,
+                   gram_ref, states_ref, ids_ref, copy_sem):
     states_copy = pltpu.make_async_copy(states_hbm, states_ref, copy_sem.at[0])
     ids_copy = pltpu.make_async_copy(ids_hbm, ids_ref, copy_sem.at[1])
     states_copy.start()
     ids_copy.start()
+    gram_copies = [
+        pltpu.make_async_copy(gram_hbm.at[b], gram_ref.at[b], copy_sem.at[2 + b]) for b in range(gram_ref.shape[0])
+    ]
+    for copy in gram_copies:
+        copy.start()
     boxes, members, _ = gram_ref.shape
     fields, cells, _ = states_ref.shape
     rows = lax.broadcasted_iota(jnp.int32, (members, members), 0)
@@ -292,9 +309,20 @@
     identity = (rows == columns).astype(jnp.float32)
     ridge = members - 1.0
 
+    states_copy.wait()
+    ids_copy.wait()
+    wide = states_ref[...].astype(jnp.float32).reshape(fields * cells, members)
+    smean = jnp.sum(wide, axis=1, keepdims=True) * (1.0 / members)
+    anomaly = (wide - smean).astype(jnp.bfloat16)
+    here = lax.broadcasted_iota(jnp.int32, (cells, cells), 0) == lax.broadcasted_iota(jnp.int32, (cells, cells), 1)
+    spread = jnp.broadcast_to(ids_ref[...].astype(jnp.float32), (cells, cells))
+    ids = jnp.sum(jnp.where(here, spread, 0.0), axis=1, keepdims=True)
+    ids = jnp.concatenate([ids] * fields, axis=0)
+
     worst = jnp.float32(0.0)
     errors = []
     for b in range(boxes):
+        gram_copies[b].wait()
         full = gram_ref[b] + ridge * identity
         top = jnp.maximum(jnp.max(jnp.sum(jnp.abs(full), axis=0, keepdims=True)), ridge)
         first = 2.0 / (top + ridge)
@@ -363,15 +391,6 @@
     def _():
         lax.while_loop(above(1e-6), refine(dot_full), tuple(errors))
 
-    states_copy.wait()
-    ids_copy.wait()
-    wide = states_ref[...].astype(jnp.float32).reshape(fields * cells, members)
-    smean = jnp.sum(wide, axis=1, keepdims=True) * (1.0 / members)
-    anomaly = (wide - smean).astype(jnp.bfloat16)
-    here = lax.broadcasted_iota(jnp.int32, (cells, cells), 0) == lax.broadcasted_iota(jnp.int32, (cells, cells), 1)
-    spread = jnp.broadcast_to(ids_ref[...].astype(jnp.float32), (cells, cells))
-    ids = jnp.sum(jnp.where(here, spread, 0.0), axis=1, keepdims=True)
-    ids = jnp.concatenate([ids] * fields, axis=0)
     total = jnp.zeros((fields * cells, members), jnp.float32)
     for b in range(boxes):
         inverse = answer[b]
@@ -388,16 +407,20 @@
     return pl.pallas_call(
         analyse_kernel,
         out_shape=jax.ShapeDtypeStruct(states.shape, jnp.bfloat16),
-        in_specs=[pl.BlockSpec(memory_space=pltpu.VMEM)] * 2 + [pl.BlockSpec(memory_space=pl.ANY)] * 2,
+        in_specs=[
+            pl.BlockSpec(memory_space=pl.ANY), pl.BlockSpec(memory_space=pltpu.VMEM),
+            pl.BlockSpec(memory_space=pl.ANY), pl.BlockSpec(memory_space=pl.ANY),
+        ],
         out_specs=pl.BlockSpec(memory_space=pltpu.VMEM),
         scratch_shapes=[
             pltpu.VMEM(square, jnp.bfloat16),
             pltpu.VMEM(square, jnp.bfloat16),
             pltpu.VMEM(square, jnp.bfloat16),
             pltpu.VMEM(square, jnp.float32),
+            pltpu.VMEM(square, jnp.float32),
             pltpu.VMEM(states.shape, jnp.bfloat16),
             pltpu.VMEM((1, box_ids.shape[0]), jnp.int32),
-            pltpu.SemaphoreType.DMA((2,)),
+            pltpu.SemaphoreType.DMA((2 + boxes,)),
         ],
         compiler_params=pltpu.CompilerParams(vmem_limit_bytes=56 * 1024 * 1024),
         name="analyse",

time: 59.7 us -> 60.3 us (1.010)
  no operation moved by 1% of the time
where the time goes in v5:
time: 60.3 us; the launch traced here: 59.3 us
  Pallas kernels  59.1 us (98%)
    pallas_call x1, Pallas kernels, gathered_sums(): pl.pallas_call(functools.partial(gather_kernel, regions, tiles), out_shap...  31.6 us
    pallas_call x1, Pallas kernels, analyse(): pl.pallas_call(analyse_kernel, out_shape=jax.ShapeDtypeStruct(states.shap...  27.5 us

profile of v5, /device:TPU:0, one launch (start us, length us, event | category | flops | bytes accessed | tf_op | source)
XLA Modules:
  0.0 59.3 jit_solution(12341027703813360424)
XLA Ops:
  0.0 31.6 %gather_gram.1 = (f32[2,512,512]{2,1,0:T(8,128)}, f32[2,512]{1,0:T(2,128)}) custom-call(bf16[128,512]{1,0:T(8,128)(2,1)} %ens_hbm.1, f32[1,128]{1,0:T(1,128)} %bitcast.6, f32[1,128]{1,0:T(1,128)} %bitcast.7, s32[1,32]{1,0:T(1,128)} %bitcast.8, s32[1,32]{1,0:T(1,128)} %bitcast.9, f32[2,2048]{1,0:T(2,128)} %local_hbm.1, f32[2,1024]{1,0:T(2,128)} %edge_hbm.1), custom_call_target="tpu_custom_call" | custom-call | tf_op jit(solution)/shard_map/gather_gram/pallas_call | solution.py:246
  31.6 27.5 %analyse.1 = bf16[2,256,512]{2,1,0:T(8,128)(2,1)} custom-call(f32[2,512,512]{2,1,0:T(8,128)} %get-tuple-element.7.gram_hbm, f32[2,512]{1,0:T(2,128)} %get-tuple-element.8.innov_ref, bf16[2,256,512]{2,1,0:T(8,128)(2,1)} %states_hbm.1, s32[1,256]{1,0:T(1,128)} %bitcast.5), custom_call_target="tpu_custom_call" | custom-call | tf_op jit(solution)/shard_map/analyse/pallas_call | solution.py:407

commit v6 on v5

--- a/solution.py
+++ b/solution.py
@@ -44,7 +44,7 @@
 
     x_others = [at_y * x_side + (at_x + d) % x_side for d in range(1, x_side)]
     y_others = [(at_y + d) % y_side * x_side + at_x for d in range(1, y_side)]
-    z_others = [(at_z + d) % z_side for d in range(1, z_side)]
+    z_others = [at_z + 1 - 2 * (at_z % 2), (at_z + 2) % z_side, z_side - 1 - at_z]
     if sides == 1:
         partners = [1 - region]
     else:
@@ -190,11 +190,10 @@
         info = jnp.concatenate(info, axis=1)
         add(data, info[0:1], info[1:2], jnp.concatenate(loc, axis=1))
 
-    order = [(at_z + z_side - d) % z_side for d in range(1, z_side)]
-    for z in order:
+    for z in z_others:
         await_piece(at, z)
         spread(z)
-    order = [at_z] + order
+    order = [at_z] + z_others
     near_units([(at, z) for z in order])
     for z in order:
         for p in x_others:
@@ -291,17 +290,12 @@
     return error * error / (2.0 - error * error)
 
 
-def analyse_kernel(gram_hbm, innov_ref, states_hbm, ids_hbm, out_ref, system_high, system_low, guess, answer,
-                   gram_ref, states_ref, ids_ref, copy_sem):
+def analyse_kernel(gram_ref, innov_ref, states_hbm, ids_hbm, out_ref, system_high, system_low, guess, answer,
+                   states_ref, ids_ref, copy_sem):
     states_copy = pltpu.make_async_copy(states_hbm, states_ref, copy_sem.at[0])
     ids_copy = pltpu.make_async_copy(ids_hbm, ids_ref, copy_sem.at[1])
     states_copy.start()
     ids_copy.start()
-    gram_copies = [
-        pltpu.make_async_copy(gram_hbm.at[b], gram_ref.at[b], copy_sem.at[2 + b]) for b in range(gram_ref.shape[0])
-    ]
-    for copy in gram_copies:
-        copy.start()
     boxes, members, _ = gram_ref.shape
     fields, cells, _ = states_ref.shape
     rows = lax.broadcasted_iota(jnp.int32, (members, members), 0)
@@ -309,20 +303,9 @@
     identity = (rows == columns).astype(jnp.float32)
     ridge = members - 1.0
 
-    states_copy.wait()
-    ids_copy.wait()
-    wide = states_ref[...].astype(jnp.float32).reshape(fields * cells, members)
-    smean = jnp.sum(wide, axis=1, keepdims=True) * (1.0 / members)
-    anomaly = (wide - smean).astype(jnp.bfloat16)
-    here = lax.broadcasted_iota(jnp.int32, (cells, cells), 0) == lax.broadcasted_iota(jnp.int32, (cells, cells), 1)
-    spread = jnp.broadcast_to(ids_ref[...].astype(jnp.float32), (cells, cells))
-    ids = jnp.sum(jnp.where(here, spread, 0.0), axis=1, keepdims=True)
-    ids = jnp.concatenate([ids] * fields, axis=0)
-
     worst = jnp.float32(0.0)
     errors = []
     for b in range(boxes):
-        gram_copies[b].wait()
         full = gram_ref[b] + ridge * identity
         top = jnp.maximum(jnp.max(jnp.sum(jnp.abs(full), axis=0, keepdims=True)), ridge)
         first = 2.0 / (top + ridge)
@@ -391,6 +374,15 @@
     def _():
         lax.while_loop(above(1e-6), refine(dot_full), tuple(errors))
 
+    states_copy.wait()
+    ids_copy.wait()
+    wide = states_ref[...].astype(jnp.float32).reshape(fields * cells, members)
+    smean = jnp.sum(wide, axis=1, keepdims=True) * (1.0 / members)
+    anomaly = (wide - smean).astype(jnp.bfloat16)
+    here = lax.broadcasted_iota(jnp.int32, (cells, cells), 0) == lax.broadcasted_iota(jnp.int32, (cells, cells), 1)
+    spread = jnp.broadcast_to(ids_ref[...].astype(jnp.float32), (cells, cells))
+    ids = jnp.sum(jnp.where(here, spread, 0.0), axis=1, keepdims=True)
+    ids = jnp.concatenate([ids] * fields, axis=0)
     total = jnp.zeros((fields * cells, members), jnp.float32)
     for b in range(boxes):
         inverse = answer[b]
@@ -407,20 +399,16 @@
     return pl.pallas_call(
         analyse_kernel,
         out_shape=jax.ShapeDtypeStruct(states.shape, jnp.bfloat16),
-        in_specs=[
-            pl.BlockSpec(memory_space=pl.ANY), pl.BlockSpec(memory_space=pltpu.VMEM),
-            pl.BlockSpec(memory_space=pl.ANY), pl.BlockSpec(memory_space=pl.ANY),
-        ],
+        in_specs=[pl.BlockSpec(memory_space=pltpu.VMEM)] * 2 + [pl.BlockSpec(memory_space=pl.ANY)] * 2,
         out_specs=pl.BlockSpec(memory_space=pltpu.VMEM),
         scratch_shapes=[
             pltpu.VMEM(square, jnp.bfloat16),
             pltpu.VMEM(square, jnp.bfloat16),
             pltpu.VMEM(square, jnp.bfloat16),
             pltpu.VMEM(square, jnp.float32),
-            pltpu.VMEM(square, jnp.float32),
             pltpu.VMEM(states.shape, jnp.bfloat16),
             pltpu.VMEM((1, box_ids.shape[0]), jnp.int32),
-            pltpu.SemaphoreType.DMA((2 + boxes,)),
+            pltpu.SemaphoreType.DMA((2,)),
         ],
         compiler_params=pltpu.CompilerParams(vmem_limit_bytes=56 * 1024 * 1024),
         name="analyse",

time: 60.3 us -> 59.6 us (0.988); the launches traced: 59.3 us -> 59.2 us
  no operation moved by 1% of the time
where the time goes in v6:
time: 59.6 us; the launch traced here: 59.2 us
  Pallas kernels  59 us (99%)
    pallas_call x1, Pallas kernels, gathered_sums(): pl.pallas_call(functools.partial(gather_kernel, regions, tiles), out_shap...  32.1 us
    pallas_call x1, Pallas kernels, analyse(): pl.pallas_call(analyse_kernel, out_shape=jax.ShapeDtypeStruct(states.shap...  26.9 us

profile of v6, /device:TPU:0, one launch (start us, length us, event | category | flops | bytes accessed | tf_op | source)
XLA Modules:
  0.0 59.2 jit_solution(6639753356800194593)
XLA Ops:
  0.0 32.1 %gather_gram.1 = (f32[2,512,512]{2,1,0:T(8,128)}, f32[2,512]{1,0:T(2,128)}) custom-call(bf16[128,512]{1,0:T(8,128)(2,1)} %ens_hbm.1, f32[1,128]{1,0:T(1,128)} %bitcast.6, f32[1,128]{1,0:T(1,128)} %bitcast.7, s32[1,32]{1,0:T(1,128)} %bitcast.8, s32[1,32]{1,0:T(1,128)} %bitcast.9, f32[2,2048]{1,0:T(2,128)} %local_hbm.1, f32[2,1024]{1,0:T(2,128)} %edge_hbm.1), custom_call_target="tpu_custom_call" | custom-call | tf_op jit(solution)/shard_map/gather_gram/pallas_call | solution.py:245
  32.1 26.9 %analyse.1 = bf16[2,256,512]{2,1,0:T(8,128)(2,1)} custom-call(f32[2,512,512]{2,1,0:T(8,128)} %get-tuple-element.7.gram_ref, f32[2,512]{1,0:T(2,128)} %get-tuple-element.8.innov_ref, bf16[2,256,512]{2,1,0:T(8,128)(2,1)} %states_hbm.1, s32[1,256]{1,0:T(1,128)} %bitcast.5), custom_call_target="tpu_custom_call" | custom-call | tf_op jit(solution)/shard_map/analyse/pallas_call | solution.py:399
